TPU v7x, 128 devices: a whole 4x4x4 slice. The times are simulated.
128 devices in a mesh: dp: 4 (over x), fsdp: 32 (over z, y, core).
Axes of the slice: x: 4, y: 4, z: 4, core: 2. Of those that a mesh axis runs over, the one named last changes fastest.
Arguments:
- queries: bfloat16 [131072, 512], P(('dp', 'fsdp')), parts along dimension 0
- ctx_grad: bfloat16 [131072, 512], P(('dp', 'fsdp')), parts along dimension 0, may hold values from -96 to 96
- neigh_states: bfloat16 [640, 128, 8192], P(('dp', 'fsdp')), parts along dimension 0
- key_weight: bfloat16 [32768, 512], P(('dp', 'fsdp')), parts along dimension 0
- value_weight: bfloat16 [8192, 512], P('fsdp'), may hold values from -0.0625 to 0.0625
- neighbours: int32 [2048, 2], P(('dp', 'fsdp')), parts along dimension 0, may hold values from 0 to 159, as said below
Outputs:
- context: bfloat16 [131072, 512], P(('dp', 'fsdp')), parts along dimension 0
- neigh_grad: bfloat16 [640, 128, 8192], P(('dp', 'fsdp')), parts along dimension 0
There are 4 independent parts, one for each index of `dp`. A program takes and returns all parts, laid end to end along the dimension named above; an argument that names none is the same for every part. Nothing has to cross between parts.
Inputs may be any that keep to these rules, and one draw needn't show every extreme that they name: `neighbours`: entry b names block b of neigh_states, held by fsdp index b // 5. Among the groups of one fsdp index every named block is named exactly twice, and at most 1 distinct blocks of one owner are named; some owner is named 2 * 1 times by the groups of every fsdp index.
All inputs are finite; a program needn't handle non-finite values.
Results may differ from a plain program's by a relative error of at most 0.0075.
The roundings to bfloat16 on the way count: a program that leaves them out, or rounds other values in their place, can miss the bound.
Values may be sent and summed in bfloat16 or wider, within the bound.
No kernel may reach another device: no remote copies, remote signals or barrier semaphores. Data moves between devices by JAX's collectives and lax.ppermute only.
A program may use at most 192 MiB of HBM per device.

v0:
```python
import functools
import math

import jax
import jax.numpy as jnp
from jax import lax
from jax.experimental import pallas as pl
from jax.experimental.pallas import tpu as pltpu
from jax.sharding import Mesh, PartitionSpec as P

HEAD_DIM = 128
RING = 4
UNITS = 64
BF = jnp.bfloat16
F32 = jnp.float32
VMEM_LIMIT = 60 * 1024 * 1024
NT = (((1,), (1,)), ((), ()))
TN = (((0,), (0,)), ((), ()))
ANY = pl.BlockSpec(memory_space=pl.ANY)
SMEM = pl.BlockSpec(memory_space=pltpu.SMEM)
VMEM = pl.BlockSpec(memory_space=pltpu.VMEM)
DMA = pltpu.SemaphoreType.DMA
PARAMS = pltpu.CompilerParams(vmem_limit_bytes=VMEM_LIMIT)


def shift(x, axis, by):
    return lax.ppermute(x, axis, [(i, (i + by) % RING) for i in range(RING)])


def swap(x):
    return lax.ppermute(x, "c", [(0, 1), (1, 0)])


def tie(x, after):
    return lax.optimization_barrier((x, after))[0]


def gather_small(x, axes):
    count = lax.axis_size(axes)
    return lax.all_to_all(jnp.broadcast_to(x[None], (count, *x.shape)), axes, 0, 0, tiled=True)


def relative(parts, start):
    return jnp.roll(parts, -start, axis=0)


def ring_gather(x, axis):
    half = x.shape[0] // 2
    after = shift(x, axis, -1)
    before = shift(x, axis, 1)
    far_a = shift(after[:half], axis, -1)
    far_b = shift(before[half:], axis, 1)
    return [x, after, far_a, far_b, before]


def total_of(own, others):
    for other in others:
        own = own + other.astype(F32)
    return own.astype(BF)


def unit_table(names, at_q, at_kv, c, block_count, q_first):
    groups = names.shape[1] // 2
    entries = names.shape[1]
    owner = names // block_count
    local = names % block_count
    owner_z = owner // (2 * RING)
    owner_y = (owner // 2) % RING
    owner_c = owner % 2
    owner_q, owner_kv = (owner_z, owner_y) if q_first else (owner_y, owner_z)
    column = ((owner_kv - at_kv) % RING) * 2 + (owner_c ^ c)
    offset = (owner_q - at_q) % RING
    entry = jnp.arange(entries, dtype=jnp.int32)
    earlier = entry[None, :] < entry[:, None]
    second = jnp.any((names[:, :, None] == names[:, None, :]) & earlier[None], axis=2)

    def other(x):
        return x.reshape(2 * RING, groups, 2)[:, :, ::-1].reshape(2 * RING, entries)

    requester = jnp.arange(2 * RING, dtype=jnp.int32)[:, None]
    req_offset, req_side = requester // 2, requester % 2
    mate_offset = other(offset)
    mate_unit = (((req_offset - mate_offset) % RING) * 2 + req_side) * 8 + other(column)
    mate_slot = other(owner_q) * (UNITS + 1) + mate_unit
    mate_second = other(second.astype(jnp.int32))
    group_row = requester * (groups * 64) + (entry // 2)[None, :] * 64
    columns = jnp.arange(2 * RING, dtype=jnp.int32)
    hit = (column[:, None, :] == columns[None, :, None]) & (offset == 0)[:, None, :]
    hit_a = hit & jnp.logical_not(second)[:, None, :]
    hit_b = hit & second[:, None, :]

    def pick(mask, x):
        return jnp.sum(jnp.where(mask, x[:, None, :], 0), axis=2)

    present = jnp.any(hit, axis=2)
    kv_row = columns[None, :] * (block_count * 128) + pick(hit_a, local) * 128
    unit = requester * 8 + columns[None, :]
    rows = jnp.stack(
        [
            unit,
            kv_row,
            pick(hit_a, group_row),
            pick(hit_b, group_row),
            pick(hit_a, mate_slot),
            pick(hit_a, mate_second),
            pick(hit_b, mate_slot),
            pick(hit_b, 1 - mate_second),
        ],
        axis=2,
    ).reshape(UNITS, 8)
    present = present.reshape(UNITS)
    place = jnp.arange(UNITS, dtype=jnp.int32)
    rank = jnp.sum(present[None, :] & (place[None, :] < place[:, None]), axis=1)
    count = jnp.sum(present.astype(jnp.int32))
    chosen = (rank[None, :] == place[:, None]) & present[None, :]
    packed = jnp.sum(jnp.where(chosen[:, :, None], rows[None], 0), axis=1)
    spare_q, spare_kv = 2 * RING * groups * 64, 2 * RING * block_count * 128
    spare = jnp.array([UNITS, spare_kv, spare_q, spare_q, UNITS, 0, UNITS, 0], jnp.int32)
    packed = jnp.where((place < count)[:, None], packed, spare[None, :])
    return jnp.concatenate([packed.reshape(-1), jnp.stack([count, at_q])])


def project_kernel(head, w_key, w_value, x_own, x_mate, kv, acc):
    step = pl.program_id(0)
    rows = x_own.shape[0]

    @pl.when(step == 0)
    def _():
        acc[...] = jnp.zeros_like(acc)

    weight = jnp.concatenate([w_key[...], w_value[...]], axis=1)
    acc[:rows] += jnp.dot(x_own[...], weight, preferred_element_type=F32)
    acc[rows:] += jnp.dot(x_mate[...], weight, preferred_element_type=F32)

    @pl.when(step == pl.num_programs(0) - 1)
    def _():
        kv[...] = acc[...].astype(BF)


def project(weight, head, x_own, x_mate):
    rows, feat = x_own.shape
    heads = weight.shape[1] // (2 * HEAD_DIM)
    width = 2 * HEAD_DIM
    depth = feat // 8
    x_spec = pl.BlockSpec((rows, depth), lambda k, head: (0, k))
    return pl.pallas_call(
        project_kernel,
        grid_spec=pltpu.PrefetchScalarGridSpec(
            num_scalar_prefetch=1,
            grid=(8,),
            in_specs=[
                pl.BlockSpec((depth, HEAD_DIM), lambda k, head: (k, head[0])),
                pl.BlockSpec((depth, HEAD_DIM), lambda k, head: (k, heads + head[0])),
                x_spec,
                x_spec,
            ],
            out_specs=pl.BlockSpec((2 * rows, width), lambda k, head: (0, 0)),
            scratch_shapes=[pltpu.VMEM((2 * rows, width), F32)],
        ),
        out_shape=jax.ShapeDtypeStruct((2 * rows, width), BF),
        compiler_params=PARAMS,
        name="project",
    )(head.reshape(1), weight, weight, x_own, x_mate)


def expand_kernel(*refs):
    grads, weight, out = refs[:4], refs[4], refs[5]
    cuts = [ref[:, i * HEAD_DIM : (i + 1) * HEAD_DIM] for i in range(2) for ref in grads]
    left = jnp.concatenate(cuts, axis=1)
    out[...] = lax.dot_general(left, weight[...], NT, preferred_element_type=F32).astype(BF)


def expand(grads, weight):
    rows, width = grads[0].shape
    feat = weight.shape[0]
    cols = feat // 16
    return pl.pallas_call(
        expand_kernel,
        grid=(16,),
        out_shape=jax.ShapeDtypeStruct((rows, feat), BF),
        in_specs=[pl.BlockSpec((rows, width), lambda n: (0, 0))] * 4 + [pl.BlockSpec((cols, 4 * width), lambda n: (n, 0))],
        out_specs=pl.BlockSpec((rows, cols), lambda n: (0, n)),
        compiler_params=PARAMS,
        name="expand",
    )(*grads, weight)


def piece_copies(refs, buf, sems):
    copies, start = [], 0
    for i, ref in enumerate(refs):
        size = ref.shape[0]
        copies.append(pltpu.make_async_copy(ref, buf.at[pl.ds(start, size)], sems.at[i]))
        start += size
    return copies


def load_unit(table, u, qbuf, kvbuf):
    kv_row = pl.multiple_of(table[u * 8 + 1], 128)
    row_a = pl.multiple_of(table[u * 8 + 2], 64)
    row_b = pl.multiple_of(table[u * 8 + 3], 64)
    qg = jnp.concatenate([qbuf[pl.ds(row_a, 64), :], qbuf[pl.ds(row_b, 64), :]], axis=0)
    kv = kvbuf[pl.ds(kv_row, 128), :]
    rows = (kv_row, row_a, row_b)
    return rows, qg[:, :HEAD_DIM], qg[:, HEAD_DIM:], kv[:, :HEAD_DIM], kv[:, HEAD_DIM:]


def stats_kernel(table, *refs):
    q_refs, kv_refs = refs[:5], refs[5:10]
    stats, qbuf, kvbuf, qsem, ksem = refs[10:]
    copies = piece_copies(q_refs, qbuf, qsem) + piece_copies(kv_refs, kvbuf, ksem)
    for copy in copies:
        copy.start()
    for copy in copies:
        copy.wait()
    scale = 1.0 / math.sqrt(HEAD_DIM)

    def step(i, carry):
        results = []
        for u in (2 * i, 2 * i + 1):
            _, q, g, k, v = load_unit(table, u, qbuf, kvbuf)
            scores = lax.dot_general(k, q, NT, preferred_element_type=F32) * scale
            prob_grads = lax.dot_general(v, g, NT, preferred_element_type=F32)
            top = jnp.max(scores, axis=0, keepdims=True)
            expo = jnp.exp(scores - top)
            total = jnp.sum(expo, axis=0, keepdims=True)
            drift = jnp.sum(expo * prob_grads, axis=0, keepdims=True) / total
            results.append(jnp.concatenate([top + jnp.log(total), drift], axis=0))
        for j, result in enumerate(results):
            stats[table[(2 * i + j) * 8]] = result
        return carry

    lax.fori_loop(0, (table[UNITS * 8] + 1) // 2, step, 0)


def grads_kernel(table, *refs):
    q_refs, kv_refs, stats = refs[:5], refs[5:10], refs[10]
    ctx_out, kvg_out = refs[11], refs[12:16]
    qbuf, kvbuf, sbuf, ctx_acc, kvg_acc, qsem, ksem, ssem = refs[16:]
    copies = piece_copies(q_refs, qbuf, qsem) + piece_copies(kv_refs, kvbuf, ksem)
    copies.append(pltpu.make_async_copy(stats, sbuf, ssem))
    for copy in copies:
        copy.start()
    ctx_acc[...] = jnp.zeros_like(ctx_acc)
    kvg_acc[...] = jnp.zeros_like(kvg_acc)
    for copy in copies:
        copy.wait()
    scale = 1.0 / math.sqrt(HEAD_DIM)

    def step(i, carry):
        results = []
        for u in (2 * i, 2 * i + 1):
            rows, q, g, k, v = load_unit(table, u, qbuf, kvbuf)
            scores = lax.dot_general(k, q, NT, preferred_element_type=F32) * scale
            prob_grads = lax.dot_general(v, g, NT, preferred_element_type=F32)
            mine = sbuf[table[UNITS * 8 + 1] * (UNITS + 1) + table[u * 8]]
            mate_a, mate_b = sbuf[table[u * 8 + 4]], sbuf[table[u * 8 + 6]]
            mate_a = jnp.where(table[u * 8 + 5] == 1, pltpu.roll(mate_a, 64, 1), mate_a)
            mate_b = jnp.where(table[u * 8 + 7] == 1, pltpu.roll(mate_b, 64, 1), mate_b)
            lane = lax.broadcasted_iota(jnp.int32, mate_a.shape, 1)
            mate = jnp.where(lane < 64, mate_a, mate_b)
            peak = jnp.maximum(mine[:1], mate[:1])
            part, part2 = jnp.exp(mine[:1] - peak), jnp.exp(mate[:1] - peak)
            both = part + part2
            norm = peak + jnp.log(both)
            drift = (mine[1:] * part + mate[1:] * part2) / both
            probs = jnp.exp(scores - norm)
            weights = probs.astype(BF)
            score_grads = (probs * (prob_grads - drift) * scale).astype(BF)
            ctx = lax.dot_general(weights, v, TN, preferred_element_type=F32)
            dv = jnp.dot(weights, g, preferred_element_type=F32)
            dk = jnp.dot(score_grads, q, preferred_element_type=F32)
            kvg = jnp.concatenate([dk, dv], axis=1).astype(BF).astype(F32)
            results.append((rows, ctx, kvg))
        for (kv_row, row_a, row_b), ctx, kvg in results:
            ctx_acc[pl.ds(row_a, 64), :] += ctx[:64]
            ctx_acc[pl.ds(row_b, 64), :] += ctx[64:]
            kvg_acc[pl.ds(kv_row, 128), :] += kvg
        return carry

    lax.fori_loop(0, (table[UNITS * 8] + 1) // 2, step, 0)
    ctx_rows, kv_rows = ctx_out.shape[0] // RING, kvg_out[0].shape[0]
    for i in range(RING):
        row = pl.multiple_of(lax.rem(table[UNITS * 8 + 1] + i, RING) * ctx_rows, ctx_rows)
        ctx_out[pl.ds(row, ctx_rows), :] = ctx_acc[pl.ds(i * ctx_rows, ctx_rows), :].astype(BF)
        kvg_out[i][...] = kvg_acc[pl.ds(i * kv_rows, kv_rows), :].astype(kvg_out[i].dtype)


def call_stats(table, q_parts, kv_parts):
    q_rows, kv_rows, width = q_parts[0].shape[0], kv_parts[0].shape[0], q_parts[0].shape[1]
    return pl.pallas_call(
        stats_kernel,
        out_shape=jax.ShapeDtypeStruct((UNITS + 1, 2, HEAD_DIM), F32),
        in_specs=[SMEM] + [ANY] * 10,
        out_specs=VMEM,
        scratch_shapes=[
            pltpu.VMEM((4 * q_rows + 64, width), BF),
            pltpu.VMEM((4 * kv_rows + 128, width), BF),
            DMA((8,)),
            DMA((8,)),
        ],
        compiler_params=PARAMS,
        name="pair_stats",
    )(table, *q_parts, *kv_parts)


def call_grads(table, q_parts, kv_parts, stats):
    q_rows, kv_rows, width = q_parts[0].shape[0], kv_parts[0].shape[0], q_parts[0].shape[1]

    def shapes(rows, cols):
        return [jax.ShapeDtypeStruct((rows, cols), F32 if i == 0 else BF) for i in range(RING)]

    outs = pl.pallas_call(
        grads_kernel,
        out_shape=[jax.ShapeDtypeStruct((RING * q_rows, HEAD_DIM), BF)] + shapes(kv_rows, width),
        in_specs=[SMEM] + [ANY] * 11,
        out_specs=[VMEM] * 5,
        scratch_shapes=[
            pltpu.VMEM((4 * q_rows + 64, width), BF),
            pltpu.VMEM((4 * kv_rows + 128, width), BF),
            pltpu.VMEM(stats.shape, F32),
            pltpu.VMEM((4 * q_rows + 64, HEAD_DIM), F32),
            pltpu.VMEM((4 * kv_rows + 128, width), F32),
            DMA((8,)),
            DMA((8,)),
            DMA,
        ],
        compiler_params=PARAMS,
        name="pair_grads",
    )(table, *q_parts, *kv_parts, stats)
    return outs[0], outs[1:]


def on_device(queries, ctx_grad, neigh_states, key_weight, value_weight, neighbours):
    z, y, c = (lax.axis_index(name).astype(jnp.int32) for name in ("z", "y", "c"))
    block_count, block_len, feat_width = neigh_states.shape
    rows = block_count * block_len
    tokens = queries.shape[0]
    states = neigh_states.reshape(rows, feat_width)
    half = 2 * HEAD_DIM

    weight = lax.all_gather(jnp.concatenate([key_weight, value_weight], axis=1), ("z", "y", "c"), axis=0, tiled=True)

    def head(which):
        cut = [lax.dynamic_slice_in_dim(x, which * HEAD_DIM, HEAD_DIM, axis=1) for x in (queries, ctx_grad)]
        return jnp.concatenate(cut, axis=1)

    qg_swap = swap(jnp.concatenate([head(2 - 2 * c), head(3 - 2 * c)], axis=1))
    states_mate = swap(tie(states, qg_swap))
    qg = [jnp.concatenate([head(2 * c + h), qg_swap[:, h * half : (h + 1) * half]], axis=0) for h in range(2)]

    names = gather_small(neighbours.reshape(-1), ("z", "y", "c")).reshape(RING, RING, 2, -1)
    names = jnp.where(c == 0, names, names[:, :, ::-1])
    names_a = relative(lax.dynamic_index_in_dim(names, z, 0, False), y).reshape(2 * RING, -1)
    names_b = relative(lax.dynamic_index_in_dim(names, y, 1, False), z).reshape(2 * RING, -1)
    table_a = unit_table(names_a, y, z, c, block_count, False)
    table_b = unit_table(names_b, z, y, c, block_count, True)

    q_a = ring_gather(qg[0], "y")
    q_b = ring_gather(qg[1], "z")
    ready = tie(weight, (q_a[2], q_a[3], q_b[2], q_b[3]))
    kv_a = ring_gather(project(ready, 2 * c, states, states_mate), "z")
    kv_b = ring_gather(project(ready, 2 * c + 1, states, states_mate), "y")

    def totals(table, q_parts, kv_parts, axis):
        stats = call_stats(table, q_parts, kv_parts)
        return gather_small(stats, axis).reshape(-1, 2, HEAD_DIM)

    stats_a = totals(tie(table_a, kv_b[0]), q_a, kv_a, "y")
    ctx_a, kvg_a = call_grads(tie(table_a, (kv_b[2], kv_b[3])), q_a, kv_a, stats_a)
    near_a = [shift(kvg_a[1], "z", 1), shift(kvg_a[3], "z", -1)]
    table_b = tie(table_b, kvg_a[0])
    stats_b = totals(table_b, q_b, kv_b, "z")
    ctx_b, kvg_b = call_grads(tie(table_b, near_a), q_b, kv_b, stats_b)
    kvg_b = total_of(kvg_b[0], [shift(kvg_b[1], "y", 1), shift(kvg_b[3], "y", -1), shift(kvg_b[2], "y", 2)])
    kvg_a = total_of(kvg_a[0], [*near_a, shift(tie(kvg_a[2], near_a), "z", 2)])
    kvg_a, kvg_c = kvg_a[:rows], swap(kvg_a[rows:])
    kvg_b, kvg_d = kvg_b[:rows], swap(kvg_b[rows:])
    ctx_a = lax.psum_scatter(ctx_a, "y", scatter_dimension=0, tiled=True)
    ctx_b = lax.psum_scatter(ctx_b, "z", scatter_dimension=0, tiled=True)
    ctx = jnp.concatenate([ctx_a, ctx_b], axis=1)
    mine, mate = ctx[:tokens], swap(ctx[tokens:])
    context = jnp.concatenate([jnp.where(c == 0, mine, mate), jnp.where(c == 0, mate, mine)], axis=1)
    first = [jnp.where(c == 0, a, b) for a, b in ((kvg_a, kvg_c), (kvg_b, kvg_d))]
    last = [jnp.where(c == 0, b, a) for a, b in ((kvg_a, kvg_c), (kvg_b, kvg_d))]
    neigh_grad = expand(first + last, weight)
    return context, neigh_grad.reshape(block_count, block_len, feat_width)


def solution(mesh):
    parts = mesh.devices.size // (RING * RING * 2)
    fine = Mesh(mesh.devices.reshape(parts, RING, RING, 2), ("dp", "z", "y", "c"))
    every = ("dp", "z", "y", "c")
    return jax.shard_map(
        on_device,
        mesh=fine,
        in_specs=(
            P(every, None),
            P(every, None),
            P(every, None, None),
            P(every, None),
            P(("z", "y", "c"), None),
            P(every, None),
        ),
        out_specs=(P(every, None), P(every, None, None)),
        check_vma=False,
    )
```

profile of v0, /device:TPU:0, one launch (start us, length us, event | category | flops | bytes accessed | tf_op | source)
XLA Modules:
  0.0 317.4 jit_solution(17359196482045921681)
XLA Ops:
  15.2 8.4 %all-to-all-start = ((s32[32,1,32]{2,1,0:T(1,128)}), s32[32,1,32]{2,1,0:T(1,128)S(1)}, u32[]{:S(2)}, u32[]{:S(2)}) async-start(s32[32,1,32]{2,1,0:T(1,128)} %broadcast_in_dim.221), calls=%async_computation | async-start | bytes 32768 | tf_op jit(solution)/shard_map/all_to_all | solution.py:40
  24.1 6.8 %all-to-all-done = s32[32,1,32]{2,1,0:T(1,128)S(1)} async-done(((s32[32,1,32]{2,1,0:T(1,128)}), s32[32,1,32]{2,1,0:T(1,128)S(1)}, u32[]{:S(2)}, u32[]{:S(2)}) %all-to-all-start) | async-done | bytes 4128 | tf_op jit(solution)/shard_map/all_to_all | solution.py:40
  46.1 27.3 %collective-permute-done.3.refs_4_ = bf16[2048,256]{1,0:T(8,128)(2,1)} collective-permute-done((bf16[2048,256]{1,0:T(8,128)(2,1)S(1)}, bf16[2048,256]{1,0:T(8,128)(2,1)}, u32[]{:S(2)}, u32[]{:S(2)}) %collective-permute-start.3) | collective-permute-done | bytes 1048608 | tf_op jit(solution)/shard_map/ppermute | solution.py:27
  77.4 3.2 %collective-permute-start.2 = (bf16[1024,256]{1,0:T(8,128)(2,1)S(1)}, bf16[1024,256]{1,0:T(8,128)(2,1)S(1)}, u32[]{:S(2)}, u32[]{:S(2)}) collective-permute-start(bf16[1024,256]{1,0:T(8,128)(2,1)S(1)} %slice.65), channel_id=1, source_target_pairs={{0,6},{2,0},{4,2},{6,4},{1,7},{3,1},{5,3},{7,5},{8,14},{10,8},{12,... | collective-permute-start | bytes 1572872 | tf_op jit(solution)/shard_map/ppermute | solution.py:27
  84.8 3.8 %collective-permute-start.6 = (bf16[1024,256]{1,0:T(8,128)(2,1)S(1)}, bf16[1024,256]{1,0:T(8,128)(2,1)S(1)}, u32[]{:S(2)}, u32[]{:S(2)}) collective-permute-start(bf16[1024,256]{1,0:T(8,128)(2,1)S(1)} %slice.68), channel_id=1, source_target_pairs={{0,24},{8,0},{16,8},{24,16},{1,25},{9,1},{17,9},{25,17},{2,26},{10... | collective-permute-start | bytes 1572872 | tf_op jit(solution)/shard_map/ppermute | solution.py:27
  91.0 9.9 %collective-permute-done.4.refs_3_ = bf16[1024,256]{1,0:T(8,128)(2,1)S(1)} collective-permute-done((bf16[1024,256]{1,0:T(8,128)(2,1)S(1)}, bf16[1024,256]{1,0:T(8,128)(2,1)S(1)}, u32[]{:S(2)}, u32[]{:S(2)}) %collective-permute-start.4) | collective-permute-done | bytes 524320 | tf_op jit(solution)/shard_map/ppermute | solution.py:27
  102.7 5.3 %collective-permute-done.8.refs_3_ = bf16[1024,256]{1,0:T(8,128)(2,1)S(1)} collective-permute-done((bf16[1024,256]{1,0:T(8,128)(2,1)S(1)}, bf16[1024,256]{1,0:T(8,128)(2,1)S(1)}, u32[]{:S(2)}, u32[]{:S(2)}) %collective-permute-start.8) | collective-permute-done | bytes 524320 | tf_op jit(solution)/shard_map/ppermute | solution.py:27
  112.4 13.5 %project.3.refs_5_ = bf16[1280,256]{1,0:T(8,128)(2,1)} custom-call(s32[1]{0:T(128)} %bitcast.13.head, bf16[8192,1024]{1,0:T(8,128)(2,1)} %all-gather.2.cloned.1.call-done.w_key.w_value.refs_4_, bf16[8192,1024]{1,0:T(8,128)(2,1)} %all-gather.2.cloned.1.call-done.w_key.w_value.refs_4_, bf16[640,8192]{1,0:T(8,128)(2,1)} %bitcast.39, ...), custom_call_target="tpu_custom_call" | custom-call | tf_op jit(solution)/shard_map/project/pallas_call | solution.py:146
  129.3 13.5 %project.2.refs_5_ = bf16[1280,256]{1,0:T(8,128)(2,1)} custom-call(s32[1]{0:T(128)} %bitcast.11.head, bf16[8192,1024]{1,0:T(8,128)(2,1)} %all-gather.2.cloned.1.call-done.w_key.w_value.refs_4_, bf16[8192,1024]{1,0:T(8,128)(2,1)} %all-gather.2.cloned.1.call-done.w_key.w_value.refs_4_, bf16[640,8192]{1,0:T(8,128)(2,1)} %bitcast.40, ...), custom_call_target="tpu_custom_call" | custom-call | tf_op jit(solution)/shard_map/project/pallas_call | solution.py:146
  150.0 3.2 %collective-permute-start.15 = (bf16[640,256]{1,0:T(8,128)(2,1)}, bf16[640,256]{1,0:T(8,128)(2,1)}, u32[]{:S(2)}, u32[]{:S(2)}) collective-permute-start(bf16[640,256]{1,0:T(8,128)(2,1)} %slice.72), channel_id=1, source_target_pairs={{0,24},{8,0},{16,8},{24,16},{1,25},{9,1},{17,9},{25,17},{2,26},{10... | collective-permute-start | bytes 983048 | tf_op jit(solution)/shard_map/ppermute | solution.py:27
  153.2 7.3 %collective-permute-done.12.refs_9_ = bf16[1280,256]{1,0:T(8,128)(2,1)S(1)} collective-permute-done((bf16[1280,256]{1,0:T(8,128)(2,1)}, bf16[1280,256]{1,0:T(8,128)(2,1)S(1)}, u32[]{:S(2)}, u32[]{:S(2)}) %collective-permute-start.12) | collective-permute-done | bytes 655392 | tf_op jit(solution)/shard_map/ppermute | solution.py:27
  162.2 3.2 %collective-permute-start.11 = (bf16[640,256]{1,0:T(8,128)(2,1)}, bf16[640,256]{1,0:T(8,128)(2,1)S(1)}, u32[]{:S(2)}, u32[]{:S(2)}) collective-permute-start(bf16[640,256]{1,0:T(8,128)(2,1)} %slice.70), channel_id=1, source_target_pairs={{0,6},{2,0},{4,2},{6,4},{1,7},{3,1},{5,3},{7,5},{8,14},{10,8},{12,... | collective-permute-start | bytes 983048 | tf_op jit(solution)/shard_map/ppermute | solution.py:27
  167.0 9.1 %pair_stats.2 = f32[65,2,128]{2,1,0:T(2,128)} custom-call(s32[514]{0:T(1024)} %pad_add_fusion.table, bf16[2048,256]{1,0:T(8,128)(2,1)} %copy-done.1, bf16[2048,256]{1,0:T(8,128)(2,1)} %collective-permute-done.1.refs_1_, bf16[1024,256]{1,0:T(8,128)(2,1)} %copy-done.10, bf16[1024,256]{1,0:T(8,128)(2,1)} %copy-done.9, ...), custom_call_target="tpu_custom_call" | custom-call | tf_op jit(solution)/shard_map/pair_stats/pallas_call | solution.py:290
  177.7 3.4 %all-to-all-start.1 = ((f32[4,65,2,128]{3,2,1,0:T(2,128)}), f32[4,65,2,128]{3,2,1,0:T(2,128)S(1)}, u32[]{:S(2)}, u32[]{:S(2)}) async-start(f32[4,65,2,128]{3,2,1,0:T(2,128)} %broadcast_in_dim.235), calls=%async_computation.1 | async-start | bytes 532480 | tf_op jit(solution)/shard_map/all_to_all | solution.py:40
  181.3 6.6 %all-to-all-done.1 = f32[4,65,2,128]{3,2,1,0:T(2,128)S(1)} async-done(((f32[4,65,2,128]{3,2,1,0:T(2,128)}), f32[4,65,2,128]{3,2,1,0:T(2,128)S(1)}, u32[]{:S(2)}, u32[]{:S(2)}) %all-to-all-start.1) | async-done | bytes 266272 | tf_op jit(solution)/shard_map/all_to_all | solution.py:40
  188.5 16.2 %pair_grads.2 = (bf16[8192,128]{1,0:T(8,128)(2,1)}, f32[1280,256]{1,0:T(8,128)}, bf16[1280,256]{1,0:T(8,128)(2,1)}, bf16[1280,256]{1,0:T(8,128)(2,1)}, bf16[1280,256]{1,0:T(8,128)(2,1)}) custom-call(s32[514]{0:T(1024)} %pad_add_fusion.table, bf16[2048,256]{1,0:T(8,128)(2,1)} %copy-done.1, bf16[2048,256]{1,0:T(8,128)(2,1)} %collective-permute-done.1.refs_1_, ...), custom_call_target="tpu_custom_call" | custom-call | tf_op jit(solution)/shard_map/pair_grads/pallas_call | solution.py:312
  210.5 9.4 %pair_stats.3 = f32[65,2,128]{2,1,0:T(2,128)} custom-call(s32[514]{0:T(1024)} %pad_add_fusion.1.table, bf16[2048,256]{1,0:T(8,128)(2,1)} %copy-done, bf16[2048,256]{1,0:T(8,128)(2,1)} %collective-permute-done.5.refs_1_, bf16[1024,256]{1,0:T(8,128)(2,1)} %copy-done.8, bf16[1024,256]{1,0:T(8,128)(2,1)} %copy-done.7, bf16[2048,256]{1,0:T(8,128)(2,1)} %copy-done.2, ...), custom_call_target="tpu_custom_call" | custom-call | tf_op jit(solution)/shard_map/pair_stats/pallas_call | solution.py:290
  221.5 3.4 %all-to-all-start.2 = ((f32[4,65,2,128]{3,2,1,0:T(2,128)}), f32[4,65,2,128]{3,2,1,0:T(2,128)S(1)}, u32[]{:S(2)}, u32[]{:S(2)}) async-start(f32[4,65,2,128]{3,2,1,0:T(2,128)} %broadcast_in_dim.246), calls=%async_computation.3 | async-start | bytes 532480 | tf_op jit(solution)/shard_map/all_to_all | solution.py:40
  225.1 6.6 %all-to-all-done.2 = f32[4,65,2,128]{3,2,1,0:T(2,128)S(1)} async-done(((f32[4,65,2,128]{3,2,1,0:T(2,128)}), f32[4,65,2,128]{3,2,1,0:T(2,128)S(1)}, u32[]{:S(2)}, u32[]{:S(2)}) %all-to-all-start.2) | async-done | bytes 266272 | tf_op jit(solution)/shard_map/all_to_all | solution.py:40
  232.4 16.2 %pair_grads.3 = (bf16[8192,128]{1,0:T(8,128)(2,1)}, f32[1280,256]{1,0:T(8,128)}, bf16[1280,256]{1,0:T(8,128)(2,1)}, bf16[1280,256]{1,0:T(8,128)(2,1)}, bf16[1280,256]{1,0:T(8,128)(2,1)}) custom-call(s32[514]{0:T(1024)} %pad_add_fusion.1.table, bf16[2048,256]{1,0:T(8,128)(2,1)} %copy-done, bf16[2048,256]{1,0:T(8,128)(2,1)} %collective-permute-done.5.refs_1_, ...), custom_call_target="tpu_custom_call" | custom-call | tf_op jit(solution)/shard_map/pair_grads/pallas_call | solution.py:312
  248.7 3.2 %collective-permute-start.24 = (bf16[1280,256]{1,0:T(8,128)(2,1)}, bf16[1280,256]{1,0:T(8,128)(2,1)S(1)}, u32[]{:S(2)}, u32[]{:S(2)}) collective-permute-start(bf16[1280,256]{1,0:T(8,128)(2,1)} %get-tuple-element.35), channel_id=1, source_target_pairs={{0,6},{2,0},{4,2},{6,4},{1,7},{3,1},{5,3},{7,5},{8,14},{10,8},{12,... | collective-permute-start | bytes 1966088 | tf_op jit(solution)/shard_map/ppermute | solution.py:27
  251.9 3.4 %collective-permute-start.21 = (bf16[1280,256]{1,0:T(8,128)(2,1)}, bf16[1280,256]{1,0:T(8,128)(2,1)S(1)}, u32[]{:S(2)}, u32[]{:S(2)}) collective-permute-start(bf16[1280,256]{1,0:T(8,128)(2,1)} %get-tuple-element.32), channel_id=1, source_target_pairs={{0,16},{8,24},{16,0},{24,8},{1,17},{9,25},{17,1},{25,9},{2,18},{10... | collective-permute-start | bytes 1966088 | tf_op jit(solution)/shard_map/ppermute | solution.py:27
  255.3 20.7 %collective-permute-done.23 = bf16[1280,256]{1,0:T(8,128)(2,1)S(1)} collective-permute-done((bf16[1280,256]{1,0:T(8,128)(2,1)}, bf16[1280,256]{1,0:T(8,128)(2,1)S(1)}, u32[]{:S(2)}, u32[]{:S(2)}) %collective-permute-start.23) | collective-permute-done | bytes 655392 | tf_op jit(solution)/shard_map/ppermute | solution.py:27
  288.4 21.3 %expand.1 = bf16[640,8192]{1,0:T(8,128)(2,1)} custom-call(bf16[640,256]{1,0:T(8,128)(2,1)} %get-tuple-element.87.refs_0_, bf16[640,256]{1,0:T(8,128)(2,1)} %get-tuple-element.85.refs_1_, bf16[640,256]{1,0:T(8,128)(2,1)} %get-tuple-element.86.refs_2_, bf16[640,256]{1,0:T(8,128)(2,1)} %get-tuple-element.84.refs_3_, ...), custom_call_target="tpu_custom_call" | custom-call | tf_op jit(solution)/shard_map/expand/pallas_call | solution.py:177
  (231 shorter events, 77.7 us)
Async XLA Ops:
  7.2 105.2 %all-gather.2.cloned.1.call-start = ((), (), s32[]{:S(2)}) async-start(), calls=%async_computation.5 | async-start | bytes 17301504 | tf_op jit(solution)/shard_map/all_gather | solution.py:341
  14.2 98.2 %collective-permute-start.9 = (bf16[640,8192]{1,0:T(8,128)(2,1)}, bf16[640,8192]{1,0:T(8,128)(2,1)}, u32[]{:S(2)}, u32[]{:S(2)}) collective-permute-start(bf16[640,8192]{1,0:T(8,128)(2,1)} %bitcast.38), channel_id=1, source_target_pairs={{0,1},{1,0},{2,3},{3,2},{4,5},{5,4},{6,7},{7,6},{8,9},{9,8},{10,11... | collective-permute-start | bytes 31457288 | tf_op jit(solution)/shard_map/ppermute | solution.py:31
  34.9 38.5 %collective-permute-start.3 = (bf16[2048,256]{1,0:T(8,128)(2,1)S(1)}, bf16[2048,256]{1,0:T(8,128)(2,1)}, u32[]{:S(2)}, u32[]{:S(2)}) collective-permute-start(bf16[2048,256]{1,0:T(8,128)(2,1)S(1)} %pad_maximum_fusion.1.refs_0_), channel_id=1, source_target_pairs={{0,2},{2,4},{4,6},{6,0},{1,3},{3,5},{5,7},{7,1},{8,10},{10,12},{12... | collective-permute-start | bytes 3145736 | tf_op jit(solution)/shard_map/ppermute | solution.py:27
  36.3 40.0 %collective-permute-start.1 = (bf16[2048,256]{1,0:T(8,128)(2,1)S(1)}, bf16[2048,256]{1,0:T(8,128)(2,1)}, u32[]{:S(2)}, u32[]{:S(2)}) collective-permute-start(bf16[2048,256]{1,0:T(8,128)(2,1)S(1)} %pad_maximum_fusion.1.refs_0_), channel_id=1, source_target_pairs={{0,6},{2,0},{4,2},{6,4},{1,7},{3,1},{5,3},{7,5},{8,14},{10,8},{12,... | collective-permute-start | bytes 3145736 | tf_op jit(solution)/shard_map/ppermute | solution.py:27
  38.4 42.7 %collective-permute-start.7 = (bf16[2048,256]{1,0:T(8,128)(2,1)S(1)}, bf16[2048,256]{1,0:T(8,128)(2,1)S(1)}, u32[]{:S(2)}, u32[]{:S(2)}) collective-permute-start(bf16[2048,256]{1,0:T(8,128)(2,1)S(1)} %pad_maximum_fusion.2.refs_0_), channel_id=1, source_target_pairs={{0,8},{8,16},{16,24},{24,0},{1,9},{9,17},{17,25},{25,1},{2,10},{10... | collective-permute-start | bytes 3145736 | tf_op jit(solution)/shard_map/ppermute | solution.py:27
  40.0 43.7 %collective-permute-start.5 = (bf16[2048,256]{1,0:T(8,128)(2,1)S(1)}, bf16[2048,256]{1,0:T(8,128)(2,1)}, u32[]{:S(2)}, u32[]{:S(2)}) collective-permute-start(bf16[2048,256]{1,0:T(8,128)(2,1)S(1)} %pad_maximum_fusion.2.refs_0_), channel_id=1, source_target_pairs={{0,24},{8,0},{16,8},{24,16},{1,25},{9,1},{17,9},{25,17},{2,26},{10... | collective-permute-start | bytes 3145736 | tf_op jit(solution)/shard_map/ppermute | solution.py:27
  74.6 26.3 %collective-permute-start.4 = (bf16[1024,256]{1,0:T(8,128)(2,1)S(1)}, bf16[1024,256]{1,0:T(8,128)(2,1)S(1)}, u32[]{:S(2)}, u32[]{:S(2)}) collective-permute-start(bf16[1024,256]{1,0:T(8,128)(2,1)S(1)} %slice.66), channel_id=1, source_target_pairs={{0,2},{2,4},{4,6},{6,0},{1,3},{3,5},{5,7},{7,1},{8,10},{10,12},{12... | collective-permute-start | bytes 1572872 | tf_op jit(solution)/shard_map/ppermute | solution.py:27
  77.4 25.3 %collective-permute-start.2 = (bf16[1024,256]{1,0:T(8,128)(2,1)S(1)}, bf16[1024,256]{1,0:T(8,128)(2,1)S(1)}, u32[]{:S(2)}, u32[]{:S(2)}) collective-permute-start(bf16[1024,256]{1,0:T(8,128)(2,1)S(1)} %slice.65), channel_id=1, source_target_pairs={{0,6},{2,0},{4,2},{6,4},{1,7},{3,1},{5,3},{7,5},{8,14},{10,8},{12,... | collective-permute-start | bytes 1572872 | tf_op jit(solution)/shard_map/ppermute | solution.py:27
  81.1 26.9 %collective-permute-start.8 = (bf16[1024,256]{1,0:T(8,128)(2,1)S(1)}, bf16[1024,256]{1,0:T(8,128)(2,1)S(1)}, u32[]{:S(2)}, u32[]{:S(2)}) collective-permute-start(bf16[1024,256]{1,0:T(8,128)(2,1)S(1)} %slice.69), channel_id=1, source_target_pairs={{0,8},{8,16},{16,24},{24,0},{1,9},{9,17},{17,25},{25,1},{2,10},{10... | collective-permute-start | bytes 1572872 | tf_op jit(solution)/shard_map/ppermute | solution.py:27
  84.8 24.7 %collective-permute-start.6 = (bf16[1024,256]{1,0:T(8,128)(2,1)S(1)}, bf16[1024,256]{1,0:T(8,128)(2,1)S(1)}, u32[]{:S(2)}, u32[]{:S(2)}) collective-permute-start(bf16[1024,256]{1,0:T(8,128)(2,1)S(1)} %slice.68), channel_id=1, source_target_pairs={{0,24},{8,0},{16,8},{24,16},{1,25},{9,1},{17,9},{25,17},{2,26},{10... | collective-permute-start | bytes 1572872 | tf_op jit(solution)/shard_map/ppermute | solution.py:27
  126.0 22.4 %collective-permute-start.16 = (bf16[1280,256]{1,0:T(8,128)(2,1)}, bf16[1280,256]{1,0:T(8,128)(2,1)S(1)}, u32[]{:S(2)}, u32[]{:S(2)}) collective-permute-start(bf16[1280,256]{1,0:T(8,128)(2,1)} %project.3.refs_5_), channel_id=1, source_target_pairs={{0,8},{8,16},{16,24},{24,0},{1,9},{9,17},{17,25},{25,1},{2,10},{10... | collective-permute-start | bytes 1966088 | tf_op jit(solution)/shard_map/ppermute | solution.py:27
  127.1 22.1 %collective-permute-start.14 = (bf16[1280,256]{1,0:T(8,128)(2,1)}, bf16[1280,256]{1,0:T(8,128)(2,1)S(1)}, u32[]{:S(2)}, u32[]{:S(2)}) collective-permute-start(bf16[1280,256]{1,0:T(8,128)(2,1)} %project.3.refs_5_), channel_id=1, source_target_pairs={{0,24},{8,0},{16,8},{24,16},{1,25},{9,1},{17,9},{25,17},{2,26},{10... | collective-permute-start | bytes 1966088 | tf_op jit(solution)/shard_map/ppermute | solution.py:27
  143.0 18.3 %collective-permute-start.10 = (bf16[1280,256]{1,0:T(8,128)(2,1)}, bf16[1280,256]{1,0:T(8,128)(2,1)S(1)}, u32[]{:S(2)}, u32[]{:S(2)}) collective-permute-start(bf16[1280,256]{1,0:T(8,128)(2,1)} %project.2.refs_5_), channel_id=1, source_target_pairs={{0,6},{2,0},{4,2},{6,4},{1,7},{3,1},{5,3},{7,5},{8,14},{10,8},{12,... | collective-permute-start | bytes 1966088 | tf_op jit(solution)/shard_map/ppermute | solution.py:27
  161.4 19.9 %collective-permute-start.13 = (bf16[640,256]{1,0:T(8,128)(2,1)}, bf16[640,256]{1,0:T(8,128)(2,1)S(1)}, u32[]{:S(2)}, u32[]{:S(2)}) collective-permute-start(bf16[640,256]{1,0:T(8,128)(2,1)} %slice.71), channel_id=1, source_target_pairs={{0,2},{2,4},{4,6},{6,0},{1,3},{3,5},{5,7},{7,1},{8,10},{10,12},{12... | collective-permute-start | bytes 983048 | tf_op jit(solution)/shard_map/ppermute | solution.py:27
  162.2 19.1 %collective-permute-start.11 = (bf16[640,256]{1,0:T(8,128)(2,1)}, bf16[640,256]{1,0:T(8,128)(2,1)S(1)}, u32[]{:S(2)}, u32[]{:S(2)}) collective-permute-start(bf16[640,256]{1,0:T(8,128)(2,1)} %slice.70), channel_id=1, source_target_pairs={{0,6},{2,0},{4,2},{6,4},{1,7},{3,1},{5,3},{7,5},{8,14},{10,8},{12,... | collective-permute-start | bytes 983048 | tf_op jit(solution)/shard_map/ppermute | solution.py:27
  181.2 99.8 %reduce-scatter.3.cloned.1.call-start = ((), (), s32[]{:S(2)}) async-start(), calls=%async_computation.6 | async-start | bytes 2621440 | tf_op jit(solution)/shard_map/reduce_scatter | solution.py:378
  205.8 19.2 %collective-permute-start.18 = (bf16[1280,256]{1,0:T(8,128)(2,1)S(1)}, bf16[1280,256]{1,0:T(8,128)(2,1)S(1)}, u32[]{:S(2)}, u32[]{:S(2)}) collective-permute-start(bf16[1280,256]{1,0:T(8,128)(2,1)S(1)} %copy-done.22), channel_id=1, source_target_pairs={{0,8},{8,16},{16,24},{24,0},{1,9},{9,17},{17,25},{25,1},{2,10},{10... | collective-permute-start | bytes 1966088 | tf_op jit(solution)/shard_map/ppermute | solution.py:27
  206.0 19.0 %collective-permute-start.19 = (bf16[1280,256]{1,0:T(8,128)(2,1)S(1)}, bf16[1280,256]{1,0:T(8,128)(2,1)S(1)}, u32[]{:S(2)}, u32[]{:S(2)}) collective-permute-start(bf16[1280,256]{1,0:T(8,128)(2,1)S(1)} %copy-done.21), channel_id=1, source_target_pairs={{0,24},{8,0},{16,8},{24,16},{1,25},{9,1},{17,9},{25,17},{2,26},{10... | collective-permute-start | bytes 1966088 | tf_op jit(solution)/shard_map/ppermute | solution.py:27
  225.0 58.3 %reduce-scatter.5.cloned.1.call-start = ((), (), s32[]{:S(2)}) async-start(), calls=%async_computation.7 | async-start | bytes 2621440 | tf_op jit(solution)/shard_map/reduce_scatter | solution.py:379
  248.6 27.4 %collective-permute-start.23 = (bf16[1280,256]{1,0:T(8,128)(2,1)}, bf16[1280,256]{1,0:T(8,128)(2,1)S(1)}, u32[]{:S(2)}, u32[]{:S(2)}) collective-permute-start(bf16[1280,256]{1,0:T(8,128)(2,1)} %get-tuple-element.34), channel_id=1, source_target_pairs={{0,2},{2,4},{4,6},{6,0},{1,3},{3,5},{5,7},{7,1},{8,10},{10,12},{12... | collective-permute-start | bytes 1966088 | tf_op jit(solution)/shard_map/ppermute | solution.py:27
  248.7 27.3 %collective-permute-start.24 = (bf16[1280,256]{1,0:T(8,128)(2,1)}, bf16[1280,256]{1,0:T(8,128)(2,1)S(1)}, u32[]{:S(2)}, u32[]{:S(2)}) collective-permute-start(bf16[1280,256]{1,0:T(8,128)(2,1)} %get-tuple-element.35), channel_id=1, source_target_pairs={{0,6},{2,0},{4,2},{6,4},{1,7},{3,1},{5,3},{7,5},{8,14},{10,8},{12,... | collective-permute-start | bytes 1966088 | tf_op jit(solution)/shard_map/ppermute | solution.py:27
  251.9 24.1 %collective-permute-start.25 = (bf16[1280,256]{1,0:T(8,128)(2,1)S(1)}, bf16[1280,256]{1,0:T(8,128)(2,1)S(1)}, u32[]{:S(2)}, u32[]{:S(2)}) collective-permute-start(bf16[1280,256]{1,0:T(8,128)(2,1)S(1)} %copy-done.23), channel_id=1, source_target_pairs={{0,4},{2,6},{4,0},{6,2},{1,5},{3,7},{5,1},{7,3},{8,12},{10,14},{12... | collective-permute-start | bytes 1966088 | tf_op jit(solution)/shard_map/ppermute | solution.py:27
  251.9 27.9 %collective-permute-start.21 = (bf16[1280,256]{1,0:T(8,128)(2,1)}, bf16[1280,256]{1,0:T(8,128)(2,1)S(1)}, u32[]{:S(2)}, u32[]{:S(2)}) collective-permute-start(bf16[1280,256]{1,0:T(8,128)(2,1)} %get-tuple-element.32), channel_id=1, source_target_pairs={{0,16},{8,24},{16,0},{24,8},{1,17},{9,25},{17,1},{25,9},{2,18},{10... | collective-permute-start | bytes 1966088 | tf_op jit(solution)/shard_map/ppermute | solution.py:27
  284.5 25.2 %collective-permute-start.20 = (bf16[1024,256]{1,0:T(8,128)(2,1)S(1)}, bf16[1024,256]{1,0:T(8,128)(2,1)S(1)}, u32[]{:S(2)}, u32[]{:S(2)}) collective-permute-start(bf16[1024,256]{1,0:T(8,128)(2,1)S(1)} %slice.75), channel_id=1, source_target_pairs={{0,1},{1,0},{2,3},{3,2},{4,5},{5,4},{6,7},{7,6},{8,9},{9,8},{10,11... | collective-permute-start | bytes 1572872 | tf_op jit(solution)/shard_map/ppermute | solution.py:31
  (33 other events, 467.9 us)
Sparse Core Ops, SparseCore 0:
  10.8 101.5 all-gather.1
  204.9 27.9 reduce-scatter.2
  248.7 34.5 reduce-scatter.4
where the time goes:
time: 321 us; the launch traced here: 317 us
  waiting for transfers between devices  105 us (33%)
  Pallas kernels  99.2 us (31%)
  starting transfers between devices  55.9 us (17%)
  local copies, waits for them, and re-layouts  23.5 us (7%)
  other arithmetic  19.1 us (6%)
  between operations  14.4 us (4%)
    ppermute x22, waiting for transfers between devices, shift(): return lax.ppermute(x, axis, [(i, (i + by) % RING) for i in range(RING)])  78.5 us
    ppermute x22, starting transfers between devices, shift(): return lax.ppermute(x, axis, [(i, (i + by) % RING) for i in range(RING)])  40 us
    pallas_call x2, Pallas kernels, call_grads(): pl.pallas_call(grads_kernel, out_shape=[jax.ShapeDtypeStruct((RING * q_ro...  32.4 us
    pallas_call x2, Pallas kernels, project(): pl.pallas_call(project_kernel, grid_spec=pltpu.PrefetchScalarGridSpec(num...  27.1 us
    pallas_call x1, Pallas kernels, expand(): pl.pallas_call(expand_kernel, grid=(16,), out_shape=jax.ShapeDtypeStruct(...  21.3 us
    all_to_all x3, waiting for transfers between devices, gather_small(): lax.all_to_all(jnp.broadcast_to(x[None], (count, *x.shape)), axes, 0, 0,...  20 us
    pallas_call x2, Pallas kernels, call_stats(): pl.pallas_call(stats_kernel, out_shape=jax.ShapeDtypeStruct((UNITS + 1, 2...  18.5 us
    all_to_all x3, starting transfers between devices, gather_small(): lax.all_to_all(jnp.broadcast_to(x[None], (count, *x.shape)), axes, 0, 0,...  15.3 us
  transfers between devices with their start and end apart: 33, of which 16 were waited for; matrix products, arithmetic and copies ran while one was open for 12% of the time, Pallas kernels for 22%

commit v1 on v0

--- a/solution.py
+++ b/solution.py
@@ -46,17 +46,24 @@
 
 def ring_gather(x, axis):
     half = x.shape[0] // 2
-    after = shift(x, axis, -1)
-    before = shift(x, axis, 1)
-    far_a = shift(after[:half], axis, -1)
-    far_b = shift(before[half:], axis, 1)
-    return [x, after, far_a, far_b, before]
-
-
-def total_of(own, others):
-    for other in others:
-        own = own + other.astype(F32)
-    return own.astype(BF)
+    after, before = shift(x, axis, -1), shift(x, axis, 1)
+    return [x, after, shift(after[:half], axis, -1), shift(before[half:], axis, 1), before]
+
+
+def line_gather(x, axis):
+    return [x, shift(x, axis, -1), shift(x, axis, 2), shift(x, axis, 1)]
+
+
+def ring_send(parts, axis):
+    own, after, far, before = parts
+    return own, shift(after, axis, 1), shift(before, axis, -1), shift(far, axis, 2)
+
+
+def total_of(parts):
+    total = parts[0]
+    for part in parts[1:]:
+        total = total + part.astype(F32)
+    return total.astype(BF)
 
 
 def unit_table(names, at_q, at_kv, c, block_count, q_first):
@@ -81,7 +88,7 @@
     req_offset, req_side = requester // 2, requester % 2
     mate_offset = other(offset)
     mate_unit = (((req_offset - mate_offset) % RING) * 2 + req_side) * 8 + other(column)
-    mate_slot = other(owner_q) * (UNITS + 1) + mate_unit
+    mate_slot = mate_offset * (UNITS + 1) + mate_unit
     mate_second = other(second.astype(jnp.int32))
     group_row = requester * (groups * 64) + (entry // 2)[None, :] * 64
     columns = jnp.arange(2 * RING, dtype=jnp.int32)
@@ -117,7 +124,7 @@
     spare_q, spare_kv = 2 * RING * groups * 64, 2 * RING * block_count * 128
     spare = jnp.array([UNITS, spare_kv, spare_q, spare_q, UNITS, 0, UNITS, 0], jnp.int32)
     packed = jnp.where((place < count)[:, None], packed, spare[None, :])
-    return jnp.concatenate([packed.reshape(-1), jnp.stack([count, at_q])])
+    return jnp.concatenate([packed.reshape(-1), jnp.stack([count, at_q, at_kv])])
 
 
 def project_kernel(head, w_key, w_value, x_own, x_mate, kv, acc):
@@ -141,13 +148,13 @@
     rows, feat = x_own.shape
     heads = weight.shape[1] // (2 * HEAD_DIM)
     width = 2 * HEAD_DIM
-    depth = feat // 8
+    depth = feat // 4
     x_spec = pl.BlockSpec((rows, depth), lambda k, head: (0, k))
     return pl.pallas_call(
         project_kernel,
         grid_spec=pltpu.PrefetchScalarGridSpec(
             num_scalar_prefetch=1,
-            grid=(8,),
+            grid=(4,),
             in_specs=[
                 pl.BlockSpec((depth, HEAD_DIM), lambda k, head: (k, head[0])),
                 pl.BlockSpec((depth, HEAD_DIM), lambda k, head: (k, heads + head[0])),
@@ -163,26 +170,37 @@
     )(head.reshape(1), weight, weight, x_own, x_mate)
 
 
-def expand_kernel(*refs):
-    grads, weight, out = refs[:4], refs[4], refs[5]
-    cuts = [ref[:, i * HEAD_DIM : (i + 1) * HEAD_DIM] for i in range(2) for ref in grads]
-    left = jnp.concatenate(cuts, axis=1)
-    out[...] = lax.dot_general(left, weight[...], NT, preferred_element_type=F32).astype(BF)
-
-
-def expand(grads, weight):
+def expand_kernel(core, *refs):
+    grads, (weight, out, left) = refs[:4], refs[4:]
+
+    @pl.when(pl.program_id(0) == 0)
+    def _():
+        for i in range(2):
+            parts = [ref[:, i * HEAD_DIM : (i + 1) * HEAD_DIM] for ref in grads]
+            own, mate = jnp.concatenate(parts[:2], axis=1), jnp.concatenate(parts[2:], axis=1)
+            start, width = i * 4 * HEAD_DIM, 2 * HEAD_DIM
+            left[:, start : start + width] = jnp.where(core[0] == 0, own, mate)
+            left[:, start + width : start + 2 * width] = jnp.where(core[0] == 0, mate, own)
+
+    out[...] = lax.dot_general(left[...], weight[...], NT, preferred_element_type=F32).astype(BF)
+
+
+def expand(core, grads, weight):
     rows, width = grads[0].shape
     feat = weight.shape[0]
-    cols = feat // 16
+    cols = feat // 4
     return pl.pallas_call(
         expand_kernel,
-        grid=(16,),
+        grid=(4,),
         out_shape=jax.ShapeDtypeStruct((rows, feat), BF),
-        in_specs=[pl.BlockSpec((rows, width), lambda n: (0, 0))] * 4 + [pl.BlockSpec((cols, 4 * width), lambda n: (n, 0))],
+        in_specs=[SMEM]
+        + [pl.BlockSpec((rows, width), lambda n: (0, 0))] * 4
+        + [pl.BlockSpec((cols, 4 * width), lambda n: (n, 0))],
         out_specs=pl.BlockSpec((rows, cols), lambda n: (0, n)),
+        scratch_shapes=[pltpu.VMEM((rows, 4 * width), BF)],
         compiler_params=PARAMS,
         name="expand",
-    )(*grads, weight)
+    )(core.reshape(1), *grads, weight)
 
 
 def piece_copies(refs, buf, sems):
@@ -205,8 +223,8 @@
 
 
 def stats_kernel(table, *refs):
-    q_refs, kv_refs = refs[:5], refs[5:10]
-    stats, qbuf, kvbuf, qsem, ksem = refs[10:]
+    q_refs, kv_refs = refs[:5], refs[5:9]
+    stats, qbuf, kvbuf, qsem, ksem = refs[9:]
     copies = piece_copies(q_refs, qbuf, qsem) + piece_copies(kv_refs, kvbuf, ksem)
     for copy in copies:
         copy.start()
@@ -232,12 +250,12 @@
     lax.fori_loop(0, (table[UNITS * 8] + 1) // 2, step, 0)
 
 
-def grads_kernel(table, *refs):
-    q_refs, kv_refs, stats = refs[:5], refs[5:10], refs[10]
-    ctx_out, kvg_out = refs[11], refs[12:16]
-    qbuf, kvbuf, sbuf, ctx_acc, kvg_acc, qsem, ksem, ssem = refs[16:]
-    copies = piece_copies(q_refs, qbuf, qsem) + piece_copies(kv_refs, kvbuf, ksem)
-    copies.append(pltpu.make_async_copy(stats, sbuf, ssem))
+def grads_kernel(ctx_ring, kvg_ring, table, *refs):
+    q_refs, kv_refs, stat_refs, refs = refs[:5], refs[5:9], refs[9:13], refs[13:]
+    ctx_count, kvg_count = RING if ctx_ring else 1, RING if kvg_ring else 1
+    ctx_out, kvg_out, refs = refs[:ctx_count], refs[ctx_count : ctx_count + kvg_count], refs[ctx_count + kvg_count :]
+    qbuf, kvbuf, sbuf, ctx_acc, kvg_acc, qsem, ksem, ssem = refs
+    copies = piece_copies(q_refs, qbuf, qsem) + piece_copies(kv_refs, kvbuf, ksem) + piece_copies(stat_refs, sbuf, ssem)
     for copy in copies:
         copy.start()
     ctx_acc[...] = jnp.zeros_like(ctx_acc)
@@ -252,7 +270,7 @@
             rows, q, g, k, v = load_unit(table, u, qbuf, kvbuf)
             scores = lax.dot_general(k, q, NT, preferred_element_type=F32) * scale
             prob_grads = lax.dot_general(v, g, NT, preferred_element_type=F32)
-            mine = sbuf[table[UNITS * 8 + 1] * (UNITS + 1) + table[u * 8]]
+            mine = sbuf[table[u * 8]]
             mate_a, mate_b = sbuf[table[u * 8 + 4]], sbuf[table[u * 8 + 6]]
             mate_a = jnp.where(table[u * 8 + 5] == 1, pltpu.roll(mate_a, 64, 1), mate_a)
             mate_b = jnp.where(table[u * 8 + 7] == 1, pltpu.roll(mate_b, 64, 1), mate_b)
@@ -278,11 +296,14 @@
         return carry
 
     lax.fori_loop(0, (table[UNITS * 8] + 1) // 2, step, 0)
-    ctx_rows, kv_rows = ctx_out.shape[0] // RING, kvg_out[0].shape[0]
-    for i in range(RING):
-        row = pl.multiple_of(lax.rem(table[UNITS * 8 + 1] + i, RING) * ctx_rows, ctx_rows)
-        ctx_out[pl.ds(row, ctx_rows), :] = ctx_acc[pl.ds(i * ctx_rows, ctx_rows), :].astype(BF)
-        kvg_out[i][...] = kvg_acc[pl.ds(i * kv_rows, kv_rows), :].astype(kvg_out[i].dtype)
+    for outs, acc, at in ((ctx_out, ctx_acc, table[UNITS * 8 + 1]), (kvg_out, kvg_acc, table[UNITS * 8 + 2])):
+        rows = outs[0].shape[0] * len(outs) // RING
+        for i in range(RING):
+            part = acc[pl.ds(i * rows, rows), :]
+            if len(outs) == RING:
+                outs[i][...] = part.astype(outs[i].dtype)
+            else:
+                outs[0][pl.ds(pl.multiple_of(lax.rem(at + i, RING) * rows, rows), rows), :] = part.astype(BF)
 
 
 def call_stats(table, q_parts, kv_parts):
@@ -290,7 +311,7 @@
     return pl.pallas_call(
         stats_kernel,
         out_shape=jax.ShapeDtypeStruct((UNITS + 1, 2, HEAD_DIM), F32),
-        in_specs=[SMEM] + [ANY] * 10,
+        in_specs=[SMEM] + [ANY] * 9,
         out_specs=VMEM,
         scratch_shapes=[
             pltpu.VMEM((4 * q_rows + 64, width), BF),
@@ -303,31 +324,34 @@
     )(table, *q_parts, *kv_parts)
 
 
-def call_grads(table, q_parts, kv_parts, stats):
+def call_grads(table, q_parts, kv_parts, stat_parts, ctx_ring, kvg_ring):
     q_rows, kv_rows, width = q_parts[0].shape[0], kv_parts[0].shape[0], q_parts[0].shape[1]
 
-    def shapes(rows, cols):
-        return [jax.ShapeDtypeStruct((rows, cols), F32 if i == 0 else BF) for i in range(RING)]
-
+    def shapes(rows, cols, ring):
+        if ring:
+            return [jax.ShapeDtypeStruct((rows, cols), F32 if i == 0 else BF) for i in range(RING)]
+        return [jax.ShapeDtypeStruct((RING * rows, cols), BF)]
+
+    ctx_shape, kvg_shape = shapes(q_rows, HEAD_DIM, ctx_ring), shapes(kv_rows, width, kvg_ring)
     outs = pl.pallas_call(
-        grads_kernel,
-        out_shape=[jax.ShapeDtypeStruct((RING * q_rows, HEAD_DIM), BF)] + shapes(kv_rows, width),
-        in_specs=[SMEM] + [ANY] * 11,
-        out_specs=[VMEM] * 5,
+        functools.partial(grads_kernel, ctx_ring, kvg_ring),
+        out_shape=ctx_shape + kvg_shape,
+        in_specs=[SMEM] + [ANY] * 13,
+        out_specs=[VMEM] * len(ctx_shape + kvg_shape),
         scratch_shapes=[
             pltpu.VMEM((4 * q_rows + 64, width), BF),
             pltpu.VMEM((4 * kv_rows + 128, width), BF),
-            pltpu.VMEM(stats.shape, F32),
+            pltpu.VMEM((RING * (UNITS + 1), 2, HEAD_DIM), F32),
             pltpu.VMEM((4 * q_rows + 64, HEAD_DIM), F32),
             pltpu.VMEM((4 * kv_rows + 128, width), F32),
             DMA((8,)),
             DMA((8,)),
-            DMA,
+            DMA((4,)),
         ],
         compiler_params=PARAMS,
         name="pair_grads",
-    )(table, *q_parts, *kv_parts, stats)
-    return outs[0], outs[1:]
+    )(table, *q_parts, *kv_parts, *stat_parts)
+    return outs[: len(ctx_shape)], outs[len(ctx_shape) :]
 
 
 def on_device(queries, ctx_grad, neigh_states, key_weight, value_weight, neighbours):
@@ -348,41 +372,36 @@
     states_mate = swap(tie(states, qg_swap))
     qg = [jnp.concatenate([head(2 * c + h), qg_swap[:, h * half : (h + 1) * half]], axis=0) for h in range(2)]
 
-    names = gather_small(neighbours.reshape(-1), ("z", "y", "c")).reshape(RING, RING, 2, -1)
+    q_a = ring_gather(qg[0], "y")
+    q_b = ring_gather(qg[1], "z")
+    rings = (q_a[2], q_a[3], q_b[2], q_b[3])
+    names = gather_small(tie(neighbours.reshape(-1), rings), ("z", "y", "c")).reshape(RING, RING, 2, -1)
+    ready = tie(weight, names)
     names = jnp.where(c == 0, names, names[:, :, ::-1])
     names_a = relative(lax.dynamic_index_in_dim(names, z, 0, False), y).reshape(2 * RING, -1)
     names_b = relative(lax.dynamic_index_in_dim(names, y, 1, False), z).reshape(2 * RING, -1)
     table_a = unit_table(names_a, y, z, c, block_count, False)
     table_b = unit_table(names_b, z, y, c, block_count, True)
 
-    q_a = ring_gather(qg[0], "y")
-    q_b = ring_gather(qg[1], "z")
-    ready = tie(weight, (q_a[2], q_a[3], q_b[2], q_b[3]))
-    kv_a = ring_gather(project(ready, 2 * c, states, states_mate), "z")
-    kv_b = ring_gather(project(ready, 2 * c + 1, states, states_mate), "y")
-
-    def totals(table, q_parts, kv_parts, axis):
-        stats = call_stats(table, q_parts, kv_parts)
-        return gather_small(stats, axis).reshape(-1, 2, HEAD_DIM)
-
-    stats_a = totals(tie(table_a, kv_b[0]), q_a, kv_a, "y")
-    ctx_a, kvg_a = call_grads(tie(table_a, (kv_b[2], kv_b[3])), q_a, kv_a, stats_a)
-    near_a = [shift(kvg_a[1], "z", 1), shift(kvg_a[3], "z", -1)]
-    table_b = tie(table_b, kvg_a[0])
-    stats_b = totals(table_b, q_b, kv_b, "z")
-    ctx_b, kvg_b = call_grads(tie(table_b, near_a), q_b, kv_b, stats_b)
-    kvg_b = total_of(kvg_b[0], [shift(kvg_b[1], "y", 1), shift(kvg_b[3], "y", -1), shift(kvg_b[2], "y", 2)])
-    kvg_a = total_of(kvg_a[0], [*near_a, shift(tie(kvg_a[2], near_a), "z", 2)])
+    kv_a = line_gather(project(ready, 2 * c, states, states_mate), "z")
+    kv_b = line_gather(project(ready, 2 * c + 1, states, states_mate), "y")
+
+    own_a = call_stats(table_a, q_a, kv_a)
+    stats_a = line_gather(own_a, "y")
+    own_b = call_stats(tie(table_b, own_a), q_b, kv_b)
+    stats_b = line_gather(own_b, "z")
+    ctx_a, (kvg_a,) = call_grads(tie(table_a, own_b), q_a, kv_a, stats_a, True, False)
+    kvg_a = lax.psum_scatter(kvg_a, "z", scatter_dimension=0, tiled=True)
+    (ctx_b,), kvg_b = call_grads(tie(table_b, own_b), q_b, kv_b, stats_b, False, True)
+    ctx_b = lax.psum_scatter(ctx_b, "z", scatter_dimension=0, tiled=True)
+    kvg_b = total_of(ring_send(kvg_b, "y"))
+    ctx_a = ring_send(tie(ctx_a, kvg_b), "y")
     kvg_a, kvg_c = kvg_a[:rows], swap(kvg_a[rows:])
     kvg_b, kvg_d = kvg_b[:rows], swap(kvg_b[rows:])
-    ctx_a = lax.psum_scatter(ctx_a, "y", scatter_dimension=0, tiled=True)
-    ctx_b = lax.psum_scatter(ctx_b, "z", scatter_dimension=0, tiled=True)
-    ctx = jnp.concatenate([ctx_a, ctx_b], axis=1)
+    neigh_grad = expand(c, [kvg_a, kvg_b, kvg_c, kvg_d], weight)
+    ctx = jnp.concatenate([total_of(tie(ctx_a, neigh_grad)), ctx_b], axis=1)
     mine, mate = ctx[:tokens], swap(ctx[tokens:])
     context = jnp.concatenate([jnp.where(c == 0, mine, mate), jnp.where(c == 0, mate, mine)], axis=1)
-    first = [jnp.where(c == 0, a, b) for a, b in ((kvg_a, kvg_c), (kvg_b, kvg_d))]
-    last = [jnp.where(c == 0, b, a) for a, b in ((kvg_a, kvg_c), (kvg_b, kvg_d))]
-    neigh_grad = expand(first + last, weight)
     return context, neigh_grad.reshape(block_count, block_len, feat_width)
 
 

time: 321 us -> 291 us (0.907)
  Pallas kernels: 99.2 us -> 86 us
  starting transfers between devices: 55.9 us -> 48.9 us
  local copies, waits for them, and re-layouts: 23.5 us -> 17.1 us
    all_to_all x3 -> x1, waiting for transfers between devices: 20 us -> 6.93 us  [gather_small(): lax.all_to_all(jnp.broadcast_to(x[None], (count, *x.shape)), axes, 0, 0,...]
    ppermute x22 -> x26, waiting for transfers between devices: 78.5 us -> 90.2 us  [shift(): return lax.ppermute(x, axis, [(i, (i + by) % RING) for i in range(RING)])]
    all_to_all x3 -> x1, starting transfers between devices: 15.3 us -> 5.51 us  [gather_small(): lax.all_to_all(jnp.broadcast_to(x[None], (count, *x.shape)), axes, 0, 0,...]
    pallas_call x3, Pallas kernels: 53.7 us -> 45.6 us  [the longest x2 29.3 us: call_grads(): pl.pallas_call(functools.partial(grads_kernel, ctx_ring, kvg_ring), out_s...]
    select_n x2 -> x0, other arithmetic: 3.7 us -> none  [on_device(): jnp.where(c == 0, b, a)]
    broadcast_in_dim x4 -> x1, local copies, waits for them, and re-layouts: 4.02 us -> 0.61 us  [gather_small(): jnp.broadcast_to(x[None], (count, *x.shape))]
    pallas_call x2, Pallas kernels: 27.1 us -> 23.8 us  [project(): pl.pallas_call(project_kernel, grid_spec=pltpu.PrefetchScalarGridSpec(num...]
    slice x9 -> x4, local copies, waits for them, and re-layouts: 6.52 us -> 3.26 us  [the longest x2 2.15 us: ring_gather(): after[:half]]
  transfers between devices with their start and end apart: 33 -> 35, of which waited for: 16 -> 15; matrix products, arithmetic and copies ran while one was open for 12% -> 8% of each run, Pallas kernels for 22% -> 21%
where the time goes in v1:
time: 291 us; the launch traced here: 287 us
  waiting for transfers between devices  103 us (35%)
  Pallas kernels  86 us (30%)
  starting transfers between devices  48.9 us (17%)
  other arithmetic  18 us (6%)
  local copies, waits for them, and re-layouts  17.1 us (6%)
  between operations  14.4 us (5%)
    ppermute x26, waiting for transfers between devices, shift(): return lax.ppermute(x, axis, [(i, (i + by) % RING) for i in range(RING)])  90.2 us
    ppermute x26, starting transfers between devices, shift(): return lax.ppermute(x, axis, [(i, (i + by) % RING) for i in range(RING)])  42.1 us
    pallas_call x2, Pallas kernels, call_grads(): pl.pallas_call(functools.partial(grads_kernel, ctx_ring, kvg_ring), out_s...  29.3 us
    pallas_call x2, Pallas kernels, project(): pl.pallas_call(project_kernel, grid_spec=pltpu.PrefetchScalarGridSpec(num...  23.8 us
    pallas_call x2, Pallas kernels, call_stats(): pl.pallas_call(stats_kernel, out_shape=jax.ShapeDtypeStruct((UNITS + 1, 2...  16.6 us
    pallas_call x1, Pallas kernels, expand(): pl.pallas_call(expand_kernel, grid=(4,), out_shape=jax.ShapeDtypeStruct((...  16.4 us
    all_to_all x1, waiting for transfers between devices, gather_small(): lax.all_to_all(jnp.broadcast_to(x[None], (count, *x.shape)), axes, 0, 0,...  6.93 us
    unnamed x49, local copies, waits for them, and re-layouts  6.05 us
  transfers between devices with their start and end apart: 35, of which 15 were waited for; matrix products, arithmetic and copies ran while one was open for 8% of the time, Pallas kernels for 21%

profile of v1, /device:TPU:0, one launch (start us, length us, event | category | flops | bytes accessed | tf_op | source)
XLA Modules:
  0.0 287.1 jit_solution(3238212080975299389)
XLA Ops:
  9.9 2.6 collective-permute-done
  18.4 2.2 collective-permute-start.5
  20.8 27.5 %collective-permute-done.3.refs_4_ = bf16[2048,256]{1,0:T(8,128)(2,1)} collective-permute-done((bf16[2048,256]{1,0:T(8,128)(2,1)S(1)}, bf16[2048,256]{1,0:T(8,128)(2,1)}, u32[]{:S(2)}, u32[]{:S(2)}) %collective-permute-start.3) | collective-permute-done | bytes 1048608 | tf_op jit(solution)/shard_map/ppermute | solution.py:27
  50.8 3.0 %collective-permute-start.2 = (bf16[1024,256]{1,0:T(8,128)(2,1)S(1)}, bf16[1024,256]{1,0:T(8,128)(2,1)}, u32[]{:S(2)}, u32[]{:S(2)}) collective-permute-start(bf16[1024,256]{1,0:T(8,128)(2,1)S(1)} %slice.49), channel_id=1, source_target_pairs={{0,6},{2,0},{4,2},{6,4},{1,7},{3,1},{5,3},{7,5},{8,14},{10,8},{12,... | collective-permute-start | bytes 1572872 | tf_op jit(solution)/shard_map/ppermute | solution.py:27
  57.0 2.5 collective-permute-start.6
  59.5 14.0 %collective-permute-done.4.refs_3_ = bf16[1024,256]{1,0:T(8,128)(2,1)} collective-permute-done((bf16[1024,256]{1,0:T(8,128)(2,1)S(1)}, bf16[1024,256]{1,0:T(8,128)(2,1)}, u32[]{:S(2)}, u32[]{:S(2)}) %collective-permute-start.4) | collective-permute-done | bytes 524320 | tf_op jit(solution)/shard_map/ppermute | solution.py:27
  73.5 3.2 %collective-permute-done.2.refs_2_ = bf16[1024,256]{1,0:T(8,128)(2,1)} collective-permute-done((bf16[1024,256]{1,0:T(8,128)(2,1)S(1)}, bf16[1024,256]{1,0:T(8,128)(2,1)}, u32[]{:S(2)}, u32[]{:S(2)}) %collective-permute-start.2) | collective-permute-done | bytes 524320 | tf_op jit(solution)/shard_map/ppermute | solution.py:27
  76.7 4.8 %collective-permute-done.8.refs_3_ = bf16[1024,256]{1,0:T(8,128)(2,1)} collective-permute-done((bf16[1024,256]{1,0:T(8,128)(2,1)S(1)}, bf16[1024,256]{1,0:T(8,128)(2,1)}, u32[]{:S(2)}, u32[]{:S(2)}) %collective-permute-start.8) | collective-permute-done | bytes 524320 | tf_op jit(solution)/shard_map/ppermute | solution.py:27
  83.1 5.5 %all-to-all-start = ((s32[32,1,32]{2,1,0:T(1,128)}), s32[32,1,32]{2,1,0:T(1,128)S(1)}, u32[]{:S(2)}, u32[]{:S(2)}) async-start(s32[32,1,32]{2,1,0:T(1,128)} %broadcast_in_dim.207), calls=%async_computation | async-start | bytes 32768 | tf_op jit(solution)/shard_map/all_to_all | solution.py:40
  89.0 6.9 %all-to-all-done = s32[32,1,32]{2,1,0:T(1,128)S(1)} async-done(((s32[32,1,32]{2,1,0:T(1,128)}), s32[32,1,32]{2,1,0:T(1,128)S(1)}, u32[]{:S(2)}, u32[]{:S(2)}) %all-to-all-start) | async-done | bytes 4128 | tf_op jit(solution)/shard_map/all_to_all | solution.py:40
  104.9 11.9 %project.2.refs_5_ = bf16[1280,256]{1,0:T(8,128)(2,1)} custom-call(s32[1]{0:T(128)} %bitcast.19.head, bf16[8192,1024]{1,0:T(8,128)(2,1)} %all-gather.2.cloned.1.call-done.w_key.w_value.refs_4_, bf16[8192,1024]{1,0:T(8,128)(2,1)} %all-gather.2.cloned.1.call-done.w_key.w_value.refs_4_, bf16[640,8192]{1,0:T(8,128)(2,1)} %bitcast.36, ...), custom_call_target="tpu_custom_call" | custom-call | tf_op jit(solution)/shard_map/project/pallas_call | solution.py:153
  122.0 11.9 %project.3.refs_5_ = bf16[1280,256]{1,0:T(8,128)(2,1)} custom-call(s32[1]{0:T(128)} %bitcast.21.head, bf16[8192,1024]{1,0:T(8,128)(2,1)} %all-gather.2.cloned.1.call-done.w_key.w_value.refs_4_, bf16[8192,1024]{1,0:T(8,128)(2,1)} %all-gather.2.cloned.1.call-done.w_key.w_value.refs_4_, bf16[640,8192]{1,0:T(8,128)(2,1)} %bitcast.37, ...), custom_call_target="tpu_custom_call" | custom-call | tf_op jit(solution)/shard_map/project/pallas_call | solution.py:153
  135.2 2.5 collective-permute-start.14
  137.7 11.2 %collective-permute-done.12.refs_8_ = bf16[1280,256]{1,0:T(8,128)(2,1)S(1)} collective-permute-done((bf16[1280,256]{1,0:T(8,128)(2,1)}, bf16[1280,256]{1,0:T(8,128)(2,1)S(1)}, u32[]{:S(2)}, u32[]{:S(2)}) %collective-permute-start.12) | collective-permute-done | bytes 655392 | tf_op jit(solution)/shard_map/ppermute | solution.py:27
  154.4 8.6 %pair_stats.2.refs_9_ = f32[65,2,128]{2,1,0:T(2,128)} custom-call(s32[515]{0:T(1024)} %pad_add_fusion.table, bf16[2048,256]{1,0:T(8,128)(2,1)} %copy-done.1, bf16[2048,256]{1,0:T(8,128)(2,1)} %collective-permute-done.1.refs_1_, bf16[1024,256]{1,0:T(8,128)(2,1)} %collective-permute-done.2.refs_2_, bf16[1024,256]{1,0:T(8,128)(2,1)} %collective-permute-done.4.refs_3_, ...), custom_call_target="tpu_custom_call" | custom-call | tf_op jit(solution)/shard_map/pair_stats/pallas_call | solution.py:311
  163.3 2.4 collective-permute-start.17
  170.5 8.0 %pair_stats.3.refs_9_ = f32[65,2,128]{2,1,0:T(2,128)} custom-call(s32[515]{0:T(1024)} %pad_add_fusion.1.table, bf16[2048,256]{1,0:T(8,128)(2,1)} %copy-done, bf16[2048,256]{1,0:T(8,128)(2,1)} %collective-permute-done.5.refs_1_, bf16[1024,256]{1,0:T(8,128)(2,1)} %collective-permute-done.6.refs_2_, bf16[1024,256]{1,0:T(8,128)(2,1)} %collective-permute-done.8.refs_3_, ...), custom_call_target="tpu_custom_call" | custom-call | tf_op jit(solution)/shard_map/pair_stats/pallas_call | solution.py:311
  179.8 15.1 %pair_grads.2 = (f32[2048,128]{1,0:T(8,128)}, bf16[2048,128]{1,0:T(8,128)(2,1)}, bf16[2048,128]{1,0:T(8,128)(2,1)}, bf16[2048,128]{1,0:T(8,128)(2,1)}, bf16[5120,256]{1,0:T(8,128)(2,1)}) custom-call(s32[515]{0:T(1024)} %pad_add_fusion.table, bf16[2048,256]{1,0:T(8,128)(2,1)} %copy-done.1, bf16[2048,256]{1,0:T(8,128)(2,1)} %collective-permute-done.1.refs_1_, ...), custom_call_target="tpu_custom_call" | custom-call | tf_op jit(solution)/shard_map/pair_grads/pallas_call | solution.py:336
  195.8 4.1 %collective-permute-start.20 = (f32[65,2,128]{2,1,0:T(2,128)S(1)}, f32[65,2,128]{2,1,0:T(2,128)S(1)}, u32[]{:S(2)}, u32[]{:S(2)}) collective-permute-start(f32[65,2,128]{2,1,0:T(2,128)S(1)} %copy-done.14), channel_id=1, source_target_pairs={{0,16},{8,24},{16,0},{24,8},{1,17},{9,25},{17,1},{25,9},{2,18},{10... | collective-permute-start | bytes 199688 | tf_op jit(solution)/shard_map/ppermute | solution.py:27
  204.8 14.1 %pair_grads.3 = (bf16[8192,128]{1,0:T(8,128)(2,1)}, f32[1280,256]{1,0:T(8,128)}, bf16[1280,256]{1,0:T(8,128)(2,1)}, bf16[1280,256]{1,0:T(8,128)(2,1)}, bf16[1280,256]{1,0:T(8,128)(2,1)}) custom-call(s32[515]{0:T(1024)} %pad_add_fusion.1.table, bf16[2048,256]{1,0:T(8,128)(2,1)} %copy-done, bf16[2048,256]{1,0:T(8,128)(2,1)} %collective-permute-done.5.refs_1_, ...), custom_call_target="tpu_custom_call" | custom-call | tf_op jit(solution)/shard_map/pair_grads/pallas_call | solution.py:336
  223.3 15.5 %collective-permute-done.22 = bf16[1280,256]{1,0:T(8,128)(2,1)S(1)} collective-permute-done((bf16[1280,256]{1,0:T(8,128)(2,1)}, bf16[1280,256]{1,0:T(8,128)(2,1)S(1)}, u32[]{:S(2)}, u32[]{:S(2)}) %collective-permute-start.22) | collective-permute-done | bytes 655392 | tf_op jit(solution)/shard_map/ppermute | solution.py:27
  238.8 9.3 %collective-permute-done.23 = bf16[1280,256]{1,0:T(8,128)(2,1)S(1)} collective-permute-done((bf16[1280,256]{1,0:T(8,128)(2,1)}, bf16[1280,256]{1,0:T(8,128)(2,1)S(1)}, u32[]{:S(2)}, u32[]{:S(2)}) %collective-permute-start.23) | collective-permute-done | bytes 655392 | tf_op jit(solution)/shard_map/ppermute | solution.py:27
  250.5 2.6 collective-permute-start.26
  258.6 16.4 %expand.1 = bf16[640,8192]{1,0:T(8,128)(2,1)} custom-call(s32[1]{0:T(128)} %bitcast.22.core, bf16[640,256]{1,0:T(8,128)(2,1)} %get-tuple-element.97.refs_0_, bf16[640,256]{1,0:T(8,128)(2,1)} %get-tuple-element.95.refs_1_, bf16[640,256]{1,0:T(8,128)(2,1)} %copy-done.13, bf16[640,256]{1,0:T(8,128)(2,1)} %copy-done.12, ...), custom_call_target="tpu_custom_call" | custom-call | tf_op jit(solution)/shard_map/expand/pallas_call | solution.py:192
  (216 shorter events, 66.9 us)
Async XLA Ops:
  7.2 97.7 %all-gather.2.cloned.1.call-start = ((), (), s32[]{:S(2)}) async-start(), calls=%async_computation.3 | async-start | bytes 17301504 | tf_op jit(solution)/shard_map/all_gather | solution.py:365
  12.6 92.3 %collective-permute-start.9 = (bf16[640,8192]{1,0:T(8,128)(2,1)}, bf16[640,8192]{1,0:T(8,128)(2,1)}, u32[]{:S(2)}, u32[]{:S(2)}) collective-permute-start(bf16[640,8192]{1,0:T(8,128)(2,1)} %bitcast.35), channel_id=1, source_target_pairs={{0,1},{1,0},{2,3},{3,2},{4,5},{5,4},{6,7},{7,6},{8,9},{9,8},{10,11... | collective-permute-start | bytes 31457288 | tf_op jit(solution)/shard_map/ppermute | solution.py:31
  12.9 35.4 %collective-permute-start.3 = (bf16[2048,256]{1,0:T(8,128)(2,1)S(1)}, bf16[2048,256]{1,0:T(8,128)(2,1)}, u32[]{:S(2)}, u32[]{:S(2)}) collective-permute-start(bf16[2048,256]{1,0:T(8,128)(2,1)S(1)} %pad_maximum_fusion.1.refs_0_), channel_id=1, source_target_pairs={{0,2},{2,4},{4,6},{6,0},{1,3},{3,5},{5,7},{7,1},{8,10},{10,12},{12... | collective-permute-start | bytes 3145736 | tf_op jit(solution)/shard_map/ppermute | solution.py:27
  14.6 35.1 %collective-permute-start.1 = (bf16[2048,256]{1,0:T(8,128)(2,1)S(1)}, bf16[2048,256]{1,0:T(8,128)(2,1)}, u32[]{:S(2)}, u32[]{:S(2)}) collective-permute-start(bf16[2048,256]{1,0:T(8,128)(2,1)S(1)} %pad_maximum_fusion.1.refs_0_), channel_id=1, source_target_pairs={{0,6},{2,0},{4,2},{6,4},{1,7},{3,1},{5,3},{7,5},{8,14},{10,8},{12,... | collective-permute-start | bytes 3145736 | tf_op jit(solution)/shard_map/ppermute | solution.py:27
  16.3 37.5 %collective-permute-start.7 = (bf16[2048,256]{1,0:T(8,128)(2,1)S(1)}, bf16[2048,256]{1,0:T(8,128)(2,1)S(1)}, u32[]{:S(2)}, u32[]{:S(2)}) collective-permute-start(bf16[2048,256]{1,0:T(8,128)(2,1)S(1)} %pad_maximum_fusion.2.refs_0_), channel_id=1, source_target_pairs={{0,8},{8,16},{16,24},{24,0},{1,9},{9,17},{17,25},{25,1},{2,10},{10... | collective-permute-start | bytes 3145736 | tf_op jit(solution)/shard_map/ppermute | solution.py:27
  18.4 37.5 %collective-permute-start.5 = (bf16[2048,256]{1,0:T(8,128)(2,1)S(1)}, bf16[2048,256]{1,0:T(8,128)(2,1)}, u32[]{:S(2)}, u32[]{:S(2)}) collective-permute-start(bf16[2048,256]{1,0:T(8,128)(2,1)S(1)} %pad_maximum_fusion.2.refs_0_), channel_id=1, source_target_pairs={{0,24},{8,0},{16,8},{24,16},{1,25},{9,1},{17,9},{25,17},{2,26},{10... | collective-permute-start | bytes 3145736 | tf_op jit(solution)/shard_map/ppermute | solution.py:27
  49.4 24.2 %collective-permute-start.4 = (bf16[1024,256]{1,0:T(8,128)(2,1)S(1)}, bf16[1024,256]{1,0:T(8,128)(2,1)}, u32[]{:S(2)}, u32[]{:S(2)}) collective-permute-start(bf16[1024,256]{1,0:T(8,128)(2,1)S(1)} %slice.50), channel_id=1, source_target_pairs={{0,2},{2,4},{4,6},{6,0},{1,3},{3,5},{5,7},{7,1},{8,10},{10,12},{12... | collective-permute-start | bytes 1572872 | tf_op jit(solution)/shard_map/ppermute | solution.py:27
  50.8 25.9 %collective-permute-start.2 = (bf16[1024,256]{1,0:T(8,128)(2,1)S(1)}, bf16[1024,256]{1,0:T(8,128)(2,1)}, u32[]{:S(2)}, u32[]{:S(2)}) collective-permute-start(bf16[1024,256]{1,0:T(8,128)(2,1)S(1)} %slice.49), channel_id=1, source_target_pairs={{0,6},{2,0},{4,2},{6,4},{1,7},{3,1},{5,3},{7,5},{8,14},{10,8},{12,... | collective-permute-start | bytes 1572872 | tf_op jit(solution)/shard_map/ppermute | solution.py:27
  53.9 27.6 %collective-permute-start.8 = (bf16[1024,256]{1,0:T(8,128)(2,1)S(1)}, bf16[1024,256]{1,0:T(8,128)(2,1)}, u32[]{:S(2)}, u32[]{:S(2)}) collective-permute-start(bf16[1024,256]{1,0:T(8,128)(2,1)S(1)} %slice.53), channel_id=1, source_target_pairs={{0,8},{8,16},{16,24},{24,0},{1,9},{9,17},{17,25},{25,1},{2,10},{10... | collective-permute-start | bytes 1572872 | tf_op jit(solution)/shard_map/ppermute | solution.py:27
  57.0 25.5 %collective-permute-start.6 = (bf16[1024,256]{1,0:T(8,128)(2,1)S(1)}, bf16[1024,256]{1,0:T(8,128)(2,1)}, u32[]{:S(2)}, u32[]{:S(2)}) collective-permute-start(bf16[1024,256]{1,0:T(8,128)(2,1)S(1)} %slice.52), channel_id=1, source_target_pairs={{0,24},{8,0},{16,8},{24,16},{1,25},{9,1},{17,9},{25,17},{2,26},{10... | collective-permute-start | bytes 1572872 | tf_op jit(solution)/shard_map/ppermute | solution.py:27
  88.6 165.7 %reduce-scatter.3.cloned.1.call-start = ((), (), s32[]{:S(2)}) async-start(), calls=%async_computation.4 | async-start | bytes 3276800 | tf_op jit(solution)/shard_map/reduce_scatter | solution.py:394
  116.8 32.0 %collective-permute-start.12 = (bf16[1280,256]{1,0:T(8,128)(2,1)}, bf16[1280,256]{1,0:T(8,128)(2,1)S(1)}, u32[]{:S(2)}, u32[]{:S(2)}) collective-permute-start(bf16[1280,256]{1,0:T(8,128)(2,1)} %project.2.refs_5_), channel_id=1, source_target_pairs={{0,8},{8,16},{16,24},{24,0},{1,9},{9,17},{17,25},{25,1},{2,10},{10... | collective-permute-start | bytes 1966088 | tf_op jit(solution)/shard_map/ppermute | solution.py:27
  118.6 35.0 %collective-permute-start.11 = (bf16[1280,256]{1,0:T(8,128)(2,1)}, bf16[1280,256]{1,0:T(8,128)(2,1)S(1)}, u32[]{:S(2)}, u32[]{:S(2)}) collective-permute-start(bf16[1280,256]{1,0:T(8,128)(2,1)} %project.2.refs_5_), channel_id=1, source_target_pairs={{0,16},{8,24},{16,0},{24,8},{1,17},{9,25},{17,1},{25,9},{2,18},{10... | collective-permute-start | bytes 1966088 | tf_op jit(solution)/shard_map/ppermute | solution.py:27
  120.7 32.8 %collective-permute-start.10 = (bf16[1280,256]{1,0:T(8,128)(2,1)}, bf16[1280,256]{1,0:T(8,128)(2,1)}, u32[]{:S(2)}, u32[]{:S(2)}) collective-permute-start(bf16[1280,256]{1,0:T(8,128)(2,1)} %project.2.refs_5_), channel_id=1, source_target_pairs={{0,24},{8,0},{16,8},{24,16},{1,25},{9,1},{17,9},{25,17},{2,26},{10... | collective-permute-start | bytes 1966088 | tf_op jit(solution)/shard_map/ppermute | solution.py:27
  133.9 31.8 %collective-permute-start.15 = (bf16[1280,256]{1,0:T(8,128)(2,1)}, bf16[1280,256]{1,0:T(8,128)(2,1)S(1)}, u32[]{:S(2)}, u32[]{:S(2)}) collective-permute-start(bf16[1280,256]{1,0:T(8,128)(2,1)} %project.3.refs_5_), channel_id=1, source_target_pairs={{0,2},{2,4},{4,6},{6,0},{1,3},{3,5},{5,7},{7,1},{8,10},{10,12},{12... | collective-permute-start | bytes 1966088 | tf_op jit(solution)/shard_map/ppermute | solution.py:27
  135.2 33.6 %collective-permute-start.14 = (bf16[1280,256]{1,0:T(8,128)(2,1)}, bf16[1280,256]{1,0:T(8,128)(2,1)S(1)}, u32[]{:S(2)}, u32[]{:S(2)}) collective-permute-start(bf16[1280,256]{1,0:T(8,128)(2,1)} %project.3.refs_5_), channel_id=1, source_target_pairs={{0,4},{2,6},{4,0},{6,2},{1,5},{3,7},{5,1},{7,3},{8,12},{10,14},{12... | collective-permute-start | bytes 1966088 | tf_op jit(solution)/shard_map/ppermute | solution.py:27
  148.8 20.0 %collective-permute-start.13 = (bf16[1280,256]{1,0:T(8,128)(2,1)}, bf16[1280,256]{1,0:T(8,128)(2,1)S(1)}, u32[]{:S(2)}, u32[]{:S(2)}) collective-permute-start(bf16[1280,256]{1,0:T(8,128)(2,1)} %project.3.refs_5_), channel_id=1, source_target_pairs={{0,6},{2,0},{4,2},{6,4},{1,7},{3,1},{5,3},{7,5},{8,14},{10,8},{12,... | collective-permute-start | bytes 1966088 | tf_op jit(solution)/shard_map/ppermute | solution.py:27
  195.0 80.3 %reduce-scatter.5.cloned.1.call-start = ((), (), s32[]{:S(2)}) async-start(), calls=%async_computation.5 | async-start | bytes 2621440 | tf_op jit(solution)/shard_map/reduce_scatter | solution.py:396
  219.0 19.7 %collective-permute-start.22 = (bf16[1280,256]{1,0:T(8,128)(2,1)}, bf16[1280,256]{1,0:T(8,128)(2,1)S(1)}, u32[]{:S(2)}, u32[]{:S(2)}) collective-permute-start(bf16[1280,256]{1,0:T(8,128)(2,1)} %get-tuple-element.38), channel_id=1, source_target_pairs={{0,2},{2,4},{4,6},{6,0},{1,3},{3,5},{5,7},{7,1},{8,10},{10,12},{12... | collective-permute-start | bytes 1966088 | tf_op jit(solution)/shard_map/ppermute | solution.py:27
  220.6 27.4 %collective-permute-start.23 = (bf16[1280,256]{1,0:T(8,128)(2,1)}, bf16[1280,256]{1,0:T(8,128)(2,1)S(1)}, u32[]{:S(2)}, u32[]{:S(2)}) collective-permute-start(bf16[1280,256]{1,0:T(8,128)(2,1)} %get-tuple-element.39), channel_id=1, source_target_pairs={{0,6},{2,0},{4,2},{6,4},{1,7},{3,1},{5,3},{7,5},{8,14},{10,8},{12,... | collective-permute-start | bytes 1966088 | tf_op jit(solution)/shard_map/ppermute | solution.py:27
  222.3 27.2 %collective-permute-start.24 = (bf16[1280,256]{1,0:T(8,128)(2,1)S(1)}, bf16[1280,256]{1,0:T(8,128)(2,1)S(1)}, u32[]{:S(2)}, u32[]{:S(2)}) collective-permute-start(bf16[1280,256]{1,0:T(8,128)(2,1)S(1)} %copy-done.23), channel_id=1, source_target_pairs={{0,4},{2,6},{4,0},{6,2},{1,5},{3,7},{5,1},{7,3},{8,12},{10,14},{12... | collective-permute-start | bytes 1966088 | tf_op jit(solution)/shard_map/ppermute | solution.py:27
  249.8 25.1 %collective-permute-start.25 = (bf16[2048,128]{1,0:T(8,128)(2,1)}, bf16[2048,128]{1,0:T(8,128)(2,1)S(1)}, u32[]{:S(2)}, u32[]{:S(2)}) collective-permute-start(bf16[2048,128]{1,0:T(8,128)(2,1)} %get-tuple-element.42), channel_id=1, source_target_pairs={{0,2},{2,4},{4,6},{6,0},{1,3},{3,5},{5,7},{7,1},{8,10},{10,12},{12... | collective-permute-start | bytes 1572872 | tf_op jit(solution)/shard_map/ppermute | solution.py:27
  250.5 24.5 %collective-permute-start.26 = (bf16[2048,128]{1,0:T(8,128)(2,1)}, bf16[2048,128]{1,0:T(8,128)(2,1)S(1)}, u32[]{:S(2)}, u32[]{:S(2)}) collective-permute-start(bf16[2048,128]{1,0:T(8,128)(2,1)} %get-tuple-element.43), channel_id=1, source_target_pairs={{0,6},{2,0},{4,2},{6,4},{1,7},{3,1},{5,3},{7,5},{8,14},{10,8},{12,... | collective-permute-start | bytes 1572872 | tf_op jit(solution)/shard_map/ppermute | solution.py:27
  253.1 21.8 %collective-permute-start.27 = (bf16[2048,128]{1,0:T(8,128)(2,1)}, bf16[2048,128]{1,0:T(8,128)(2,1)S(1)}, u32[]{:S(2)}, u32[]{:S(2)}) collective-permute-start(bf16[2048,128]{1,0:T(8,128)(2,1)} %get-tuple-element.44), channel_id=1, source_target_pairs={{0,4},{2,6},{4,0},{6,2},{1,5},{3,7},{5,1},{7,3},{8,12},{10,14},{12... | collective-permute-start | bytes 1572872 | tf_op jit(solution)/shard_map/ppermute | solution.py:27
  (35 other events, 319.2 us)
Sparse Core Ops, SparseCore 0:
  10.9 92.7 all-gather.1
  195.1 35.1 reduce-scatter.2
  232.7 29.4 reduce-scatter.4

commit v2 on v1

--- a/solution.py
+++ b/solution.py
@@ -11,6 +11,7 @@
 HEAD_DIM = 128
 RING = 4
 UNITS = 64
+WAYS = 8
 BF = jnp.bfloat16
 F32 = jnp.float32
 VMEM_LIMIT = 60 * 1024 * 1024
@@ -234,7 +235,7 @@
 
     def step(i, carry):
         results = []
-        for u in (2 * i, 2 * i + 1):
+        for u in [WAYS * i + w for w in range(WAYS)]:
             _, q, g, k, v = load_unit(table, u, qbuf, kvbuf)
             scores = lax.dot_general(k, q, NT, preferred_element_type=F32) * scale
             prob_grads = lax.dot_general(v, g, NT, preferred_element_type=F32)
@@ -244,10 +245,10 @@
             drift = jnp.sum(expo * prob_grads, axis=0, keepdims=True) / total
             results.append(jnp.concatenate([top + jnp.log(total), drift], axis=0))
         for j, result in enumerate(results):
-            stats[table[(2 * i + j) * 8]] = result
+            stats[table[(WAYS * i + j) * 8]] = result
         return carry
 
-    lax.fori_loop(0, (table[UNITS * 8] + 1) // 2, step, 0)
+    lax.fori_loop(0, (table[UNITS * 8] + WAYS - 1) // WAYS, step, 0)
 
 
 def grads_kernel(ctx_ring, kvg_ring, table, *refs):
@@ -266,7 +267,7 @@
 
     def step(i, carry):
         results = []
-        for u in (2 * i, 2 * i + 1):
+        for u in [WAYS * i + w for w in range(WAYS)]:
             rows, q, g, k, v = load_unit(table, u, qbuf, kvbuf)
             scores = lax.dot_general(k, q, NT, preferred_element_type=F32) * scale
             prob_grads = lax.dot_general(v, g, NT, preferred_element_type=F32)
@@ -295,7 +296,7 @@
             kvg_acc[pl.ds(kv_row, 128), :] += kvg
         return carry
 
-    lax.fori_loop(0, (table[UNITS * 8] + 1) // 2, step, 0)
+    lax.fori_loop(0, (table[UNITS * 8] + WAYS - 1) // WAYS, step, 0)
     for outs, acc, at in ((ctx_out, ctx_acc, table[UNITS * 8 + 1]), (kvg_out, kvg_acc, table[UNITS * 8 + 2])):
         rows = outs[0].shape[0] * len(outs) // RING
         for i in range(RING):

time: 291 us -> 284 us (0.976)
  Pallas kernels: 86 us -> 80.4 us
    pallas_call x2, Pallas kernels: 16.6 us -> 13.6 us  [call_stats(): pl.pallas_call(stats_kernel, out_shape=jax.ShapeDtypeStruct((UNITS + 1, 2...]
  transfers between devices with their start and end apart: 35 -> 35, of which waited for: 15 -> 15; matrix products, arithmetic and copies ran while one was open for 8% -> 8% of each run, Pallas kernels for 21% -> 20%
where the time goes in v2:
time: 284 us; the launch traced here: 282 us
  waiting for transfers between devices  102 us (36%)
  Pallas kernels  80.4 us (28%)
  starting transfers between devices  50.9 us (18%)
  other arithmetic  18 us (6%)
  local copies, waits for them, and re-layouts  16.3 us (6%)
  between operations  14.4 us (5%)
    ppermute x26, waiting for transfers between devices, shift(): return lax.ppermute(x, axis, [(i, (i + by) % RING) for i in range(RING)])  89.6 us
    ppermute x26, starting transfers between devices, shift(): return lax.ppermute(x, axis, [(i, (i + by) % RING) for i in range(RING)])  44.1 us
    pallas_call x2, Pallas kernels, call_grads(): pl.pallas_call(functools.partial(grads_kernel, ctx_ring, kvg_ring), out_s...  26.6 us
    pallas_call x2, Pallas kernels, project(): pl.pallas_call(project_kernel, grid_spec=pltpu.PrefetchScalarGridSpec(num...  23.8 us
    pallas_call x1, Pallas kernels, expand(): pl.pallas_call(expand_kernel, grid=(4,), out_shape=jax.ShapeDtypeStruct((...  16.4 us
    pallas_call x2, Pallas kernels, call_stats(): pl.pallas_call(stats_kernel, out_shape=jax.ShapeDtypeStruct((UNITS + 1, 2...  13.6 us
    all_to_all x1, waiting for transfers between devices, gather_small(): lax.all_to_all(jnp.broadcast_to(x[None], (count, *x.shape)), axes, 0, 0,...  6.93 us
  transfers between devices with their start and end apart: 35, of which 15 were waited for; matrix products, arithmetic and copies ran while one was open for 8% of the time, Pallas kernels for 20%

profile of v2, /device:TPU:0, one launch (start us, length us, event | category | flops | bytes accessed | tf_op | source)
XLA Modules:
  0.0 282.1 jit_solution(13967673740922746912)
XLA Ops:
  9.9 2.6 collective-permute-done
  18.4 2.2 collective-permute-start.5
  20.8 27.5 %collective-permute-done.3.refs_4_ = bf16[2048,256]{1,0:T(8,128)(2,1)} collective-permute-done((bf16[2048,256]{1,0:T(8,128)(2,1)S(1)}, bf16[2048,256]{1,0:T(8,128)(2,1)}, u32[]{:S(2)}, u32[]{:S(2)}) %collective-permute-start.3) | collective-permute-done | bytes 1048608 | tf_op jit(solution)/shard_map/ppermute | solution.py:28
  50.8 3.0 %collective-permute-start.2 = (bf16[1024,256]{1,0:T(8,128)(2,1)S(1)}, bf16[1024,256]{1,0:T(8,128)(2,1)}, u32[]{:S(2)}, u32[]{:S(2)}) collective-permute-start(bf16[1024,256]{1,0:T(8,128)(2,1)S(1)} %slice.49), channel_id=1, source_target_pairs={{0,6},{2,0},{4,2},{6,4},{1,7},{3,1},{5,3},{7,5},{8,14},{10,8},{12,... | collective-permute-start | bytes 1572872 | tf_op jit(solution)/shard_map/ppermute | solution.py:28
  57.0 2.5 collective-permute-start.6
  59.5 14.0 %collective-permute-done.4.refs_3_ = bf16[1024,256]{1,0:T(8,128)(2,1)} collective-permute-done((bf16[1024,256]{1,0:T(8,128)(2,1)S(1)}, bf16[1024,256]{1,0:T(8,128)(2,1)}, u32[]{:S(2)}, u32[]{:S(2)}) %collective-permute-start.4) | collective-permute-done | bytes 524320 | tf_op jit(solution)/shard_map/ppermute | solution.py:28
  73.5 3.2 %collective-permute-done.2.refs_2_ = bf16[1024,256]{1,0:T(8,128)(2,1)} collective-permute-done((bf16[1024,256]{1,0:T(8,128)(2,1)S(1)}, bf16[1024,256]{1,0:T(8,128)(2,1)}, u32[]{:S(2)}, u32[]{:S(2)}) %collective-permute-start.2) | collective-permute-done | bytes 524320 | tf_op jit(solution)/shard_map/ppermute | solution.py:28
  76.7 4.8 %collective-permute-done.8.refs_3_ = bf16[1024,256]{1,0:T(8,128)(2,1)} collective-permute-done((bf16[1024,256]{1,0:T(8,128)(2,1)S(1)}, bf16[1024,256]{1,0:T(8,128)(2,1)}, u32[]{:S(2)}, u32[]{:S(2)}) %collective-permute-start.8) | collective-permute-done | bytes 524320 | tf_op jit(solution)/shard_map/ppermute | solution.py:28
  83.1 5.5 %all-to-all-start = ((s32[32,1,32]{2,1,0:T(1,128)}), s32[32,1,32]{2,1,0:T(1,128)S(1)}, u32[]{:S(2)}, u32[]{:S(2)}) async-start(s32[32,1,32]{2,1,0:T(1,128)} %broadcast_in_dim.207), calls=%async_computation | async-start | bytes 32768 | tf_op jit(solution)/shard_map/all_to_all | solution.py:41
  89.0 6.9 %all-to-all-done = s32[32,1,32]{2,1,0:T(1,128)S(1)} async-done(((s32[32,1,32]{2,1,0:T(1,128)}), s32[32,1,32]{2,1,0:T(1,128)S(1)}, u32[]{:S(2)}, u32[]{:S(2)}) %all-to-all-start) | async-done | bytes 4128 | tf_op jit(solution)/shard_map/all_to_all | solution.py:41
  104.9 11.9 %project.2.refs_5_ = bf16[1280,256]{1,0:T(8,128)(2,1)} custom-call(s32[1]{0:T(128)} %bitcast.19.head, bf16[8192,1024]{1,0:T(8,128)(2,1)} %all-gather.2.cloned.1.call-done.w_key.w_value.refs_4_, bf16[8192,1024]{1,0:T(8,128)(2,1)} %all-gather.2.cloned.1.call-done.w_key.w_value.refs_4_, bf16[640,8192]{1,0:T(8,128)(2,1)} %bitcast.36, ...), custom_call_target="tpu_custom_call" | custom-call | tf_op jit(solution)/shard_map/project/pallas_call | solution.py:154
  122.0 11.9 %project.3.refs_5_ = bf16[1280,256]{1,0:T(8,128)(2,1)} custom-call(s32[1]{0:T(128)} %bitcast.21.head, bf16[8192,1024]{1,0:T(8,128)(2,1)} %all-gather.2.cloned.1.call-done.w_key.w_value.refs_4_, bf16[8192,1024]{1,0:T(8,128)(2,1)} %all-gather.2.cloned.1.call-done.w_key.w_value.refs_4_, bf16[640,8192]{1,0:T(8,128)(2,1)} %bitcast.37, ...), custom_call_target="tpu_custom_call" | custom-call | tf_op jit(solution)/shard_map/project/pallas_call | solution.py:154
  135.2 2.5 collective-permute-start.14
  137.7 11.2 %collective-permute-done.12.refs_8_ = bf16[1280,256]{1,0:T(8,128)(2,1)S(1)} collective-permute-done((bf16[1280,256]{1,0:T(8,128)(2,1)}, bf16[1280,256]{1,0:T(8,128)(2,1)S(1)}, u32[]{:S(2)}, u32[]{:S(2)}) %collective-permute-start.12) | collective-permute-done | bytes 655392 | tf_op jit(solution)/shard_map/ppermute | solution.py:28
  154.4 6.5 %pair_stats.2.refs_9_ = f32[65,2,128]{2,1,0:T(2,128)} custom-call(s32[515]{0:T(1024)} %pad_add_fusion.table, bf16[2048,256]{1,0:T(8,128)(2,1)} %copy-done.1, bf16[2048,256]{1,0:T(8,128)(2,1)} %collective-permute-done.1.refs_1_, bf16[1024,256]{1,0:T(8,128)(2,1)} %collective-permute-done.2.refs_2_, bf16[1024,256]{1,0:T(8,128)(2,1)} %collective-permute-done.4.refs_3_, ...), custom_call_target="tpu_custom_call" | custom-call | tf_op jit(solution)/shard_map/pair_stats/pallas_call | solution.py:312
  168.7 7.1 %pair_stats.3.refs_9_ = f32[65,2,128]{2,1,0:T(2,128)} custom-call(s32[515]{0:T(1024)} %pad_add_fusion.1.table, bf16[2048,256]{1,0:T(8,128)(2,1)} %copy-done, bf16[2048,256]{1,0:T(8,128)(2,1)} %collective-permute-done.5.refs_1_, bf16[1024,256]{1,0:T(8,128)(2,1)} %collective-permute-done.6.refs_2_, bf16[1024,256]{1,0:T(8,128)(2,1)} %collective-permute-done.8.refs_3_, ...), custom_call_target="tpu_custom_call" | custom-call | tf_op jit(solution)/shard_map/pair_stats/pallas_call | solution.py:312
  177.1 12.5 %pair_grads.2 = (f32[2048,128]{1,0:T(8,128)}, bf16[2048,128]{1,0:T(8,128)(2,1)}, bf16[2048,128]{1,0:T(8,128)(2,1)}, bf16[2048,128]{1,0:T(8,128)(2,1)}, bf16[5120,256]{1,0:T(8,128)(2,1)}) custom-call(s32[515]{0:T(1024)} %pad_add_fusion.table, bf16[2048,256]{1,0:T(8,128)(2,1)} %copy-done.1, bf16[2048,256]{1,0:T(8,128)(2,1)} %collective-permute-done.1.refs_1_, ...), custom_call_target="tpu_custom_call" | custom-call | tf_op jit(solution)/shard_map/pair_grads/pallas_call | solution.py:337
  190.5 2.3 collective-permute-start.21
  194.3 2.6 collective-permute-start.19
  200.0 14.1 %pair_grads.3 = (bf16[8192,128]{1,0:T(8,128)(2,1)}, f32[1280,256]{1,0:T(8,128)}, bf16[1280,256]{1,0:T(8,128)(2,1)}, bf16[1280,256]{1,0:T(8,128)(2,1)}, bf16[1280,256]{1,0:T(8,128)(2,1)}) custom-call(s32[515]{0:T(1024)} %pad_add_fusion.1.table, bf16[2048,256]{1,0:T(8,128)(2,1)} %copy-done, bf16[2048,256]{1,0:T(8,128)(2,1)} %collective-permute-done.5.refs_1_, ...), custom_call_target="tpu_custom_call" | custom-call | tf_op jit(solution)/shard_map/pair_grads/pallas_call | solution.py:337
  214.2 3.0 %collective-permute-start.22 = (bf16[1280,256]{1,0:T(8,128)(2,1)}, bf16[1280,256]{1,0:T(8,128)(2,1)S(1)}, u32[]{:S(2)}, u32[]{:S(2)}) collective-permute-start(bf16[1280,256]{1,0:T(8,128)(2,1)} %get-tuple-element.38), channel_id=1, source_target_pairs={{0,2},{2,4},{4,6},{6,0},{1,3},{3,5},{5,7},{7,1},{8,10},{10,12},{12... | collective-permute-start | bytes 1966088 | tf_op jit(solution)/shard_map/ppermute | solution.py:28
  219.4 24.1 %collective-permute-done.22 = bf16[1280,256]{1,0:T(8,128)(2,1)S(1)} collective-permute-done((bf16[1280,256]{1,0:T(8,128)(2,1)}, bf16[1280,256]{1,0:T(8,128)(2,1)S(1)}, u32[]{:S(2)}, u32[]{:S(2)}) %collective-permute-start.22) | collective-permute-done | bytes 655392 | tf_op jit(solution)/shard_map/ppermute | solution.py:28
  244.7 2.4 collective-permute-start.26
  253.5 16.4 %expand.1 = bf16[640,8192]{1,0:T(8,128)(2,1)} custom-call(s32[1]{0:T(128)} %bitcast.22.core, bf16[640,256]{1,0:T(8,128)(2,1)} %get-tuple-element.97.refs_0_, bf16[640,256]{1,0:T(8,128)(2,1)} %get-tuple-element.95.refs_1_, bf16[640,256]{1,0:T(8,128)(2,1)} %copy-done.13, bf16[640,256]{1,0:T(8,128)(2,1)} %copy-done.12, ...), custom_call_target="tpu_custom_call" | custom-call | tf_op jit(solution)/shard_map/expand/pallas_call | solution.py:193
  (216 shorter events, 66.9 us)
Async XLA Ops:
  7.2 97.7 %all-gather.2.cloned.1.call-start = ((), (), s32[]{:S(2)}) async-start(), calls=%async_computation.3 | async-start | bytes 17301504 | tf_op jit(solution)/shard_map/all_gather | solution.py:366
  12.6 92.3 %collective-permute-start.9 = (bf16[640,8192]{1,0:T(8,128)(2,1)}, bf16[640,8192]{1,0:T(8,128)(2,1)}, u32[]{:S(2)}, u32[]{:S(2)}) collective-permute-start(bf16[640,8192]{1,0:T(8,128)(2,1)} %bitcast.35), channel_id=1, source_target_pairs={{0,1},{1,0},{2,3},{3,2},{4,5},{5,4},{6,7},{7,6},{8,9},{9,8},{10,11... | collective-permute-start | bytes 31457288 | tf_op jit(solution)/shard_map/ppermute | solution.py:32
  12.9 35.4 %collective-permute-start.3 = (bf16[2048,256]{1,0:T(8,128)(2,1)S(1)}, bf16[2048,256]{1,0:T(8,128)(2,1)}, u32[]{:S(2)}, u32[]{:S(2)}) collective-permute-start(bf16[2048,256]{1,0:T(8,128)(2,1)S(1)} %pad_maximum_fusion.1.refs_0_), channel_id=1, source_target_pairs={{0,2},{2,4},{4,6},{6,0},{1,3},{3,5},{5,7},{7,1},{8,10},{10,12},{12... | collective-permute-start | bytes 3145736 | tf_op jit(solution)/shard_map/ppermute | solution.py:28
  14.6 35.1 %collective-permute-start.1 = (bf16[2048,256]{1,0:T(8,128)(2,1)S(1)}, bf16[2048,256]{1,0:T(8,128)(2,1)}, u32[]{:S(2)}, u32[]{:S(2)}) collective-permute-start(bf16[2048,256]{1,0:T(8,128)(2,1)S(1)} %pad_maximum_fusion.1.refs_0_), channel_id=1, source_target_pairs={{0,6},{2,0},{4,2},{6,4},{1,7},{3,1},{5,3},{7,5},{8,14},{10,8},{12,... | collective-permute-start | bytes 3145736 | tf_op jit(solution)/shard_map/ppermute | solution.py:28
  16.3 37.5 %collective-permute-start.7 = (bf16[2048,256]{1,0:T(8,128)(2,1)S(1)}, bf16[2048,256]{1,0:T(8,128)(2,1)S(1)}, u32[]{:S(2)}, u32[]{:S(2)}) collective-permute-start(bf16[2048,256]{1,0:T(8,128)(2,1)S(1)} %pad_maximum_fusion.2.refs_0_), channel_id=1, source_target_pairs={{0,8},{8,16},{16,24},{24,0},{1,9},{9,17},{17,25},{25,1},{2,10},{10... | collective-permute-start | bytes 3145736 | tf_op jit(solution)/shard_map/ppermute | solution.py:28
  18.4 37.5 %collective-permute-start.5 = (bf16[2048,256]{1,0:T(8,128)(2,1)S(1)}, bf16[2048,256]{1,0:T(8,128)(2,1)}, u32[]{:S(2)}, u32[]{:S(2)}) collective-permute-start(bf16[2048,256]{1,0:T(8,128)(2,1)S(1)} %pad_maximum_fusion.2.refs_0_), channel_id=1, source_target_pairs={{0,24},{8,0},{16,8},{24,16},{1,25},{9,1},{17,9},{25,17},{2,26},{10... | collective-permute-start | bytes 3145736 | tf_op jit(solution)/shard_map/ppermute | solution.py:28
  49.4 24.2 %collective-permute-start.4 = (bf16[1024,256]{1,0:T(8,128)(2,1)S(1)}, bf16[1024,256]{1,0:T(8,128)(2,1)}, u32[]{:S(2)}, u32[]{:S(2)}) collective-permute-start(bf16[1024,256]{1,0:T(8,128)(2,1)S(1)} %slice.50), channel_id=1, source_target_pairs={{0,2},{2,4},{4,6},{6,0},{1,3},{3,5},{5,7},{7,1},{8,10},{10,12},{12... | collective-permute-start | bytes 1572872 | tf_op jit(solution)/shard_map/ppermute | solution.py:28
  50.8 25.9 %collective-permute-start.2 = (bf16[1024,256]{1,0:T(8,128)(2,1)S(1)}, bf16[1024,256]{1,0:T(8,128)(2,1)}, u32[]{:S(2)}, u32[]{:S(2)}) collective-permute-start(bf16[1024,256]{1,0:T(8,128)(2,1)S(1)} %slice.49), channel_id=1, source_target_pairs={{0,6},{2,0},{4,2},{6,4},{1,7},{3,1},{5,3},{7,5},{8,14},{10,8},{12,... | collective-permute-start | bytes 1572872 | tf_op jit(solution)/shard_map/ppermute | solution.py:28
  53.9 27.6 %collective-permute-start.8 = (bf16[1024,256]{1,0:T(8,128)(2,1)S(1)}, bf16[1024,256]{1,0:T(8,128)(2,1)}, u32[]{:S(2)}, u32[]{:S(2)}) collective-permute-start(bf16[1024,256]{1,0:T(8,128)(2,1)S(1)} %slice.53), channel_id=1, source_target_pairs={{0,8},{8,16},{16,24},{24,0},{1,9},{9,17},{17,25},{25,1},{2,10},{10... | collective-permute-start | bytes 1572872 | tf_op jit(solution)/shard_map/ppermute | solution.py:28
  57.0 25.5 %collective-permute-start.6 = (bf16[1024,256]{1,0:T(8,128)(2,1)S(1)}, bf16[1024,256]{1,0:T(8,128)(2,1)}, u32[]{:S(2)}, u32[]{:S(2)}) collective-permute-start(bf16[1024,256]{1,0:T(8,128)(2,1)S(1)} %slice.52), channel_id=1, source_target_pairs={{0,24},{8,0},{16,8},{24,16},{1,25},{9,1},{17,9},{25,17},{2,26},{10... | collective-permute-start | bytes 1572872 | tf_op jit(solution)/shard_map/ppermute | solution.py:28
  88.6 160.6 %reduce-scatter.3.cloned.1.call-start = ((), (), s32[]{:S(2)}) async-start(), calls=%async_computation.4 | async-start | bytes 3276800 | tf_op jit(solution)/shard_map/reduce_scatter | solution.py:395
  116.8 32.0 %collective-permute-start.12 = (bf16[1280,256]{1,0:T(8,128)(2,1)}, bf16[1280,256]{1,0:T(8,128)(2,1)S(1)}, u32[]{:S(2)}, u32[]{:S(2)}) collective-permute-start(bf16[1280,256]{1,0:T(8,128)(2,1)} %project.2.refs_5_), channel_id=1, source_target_pairs={{0,8},{8,16},{16,24},{24,0},{1,9},{9,17},{17,25},{25,1},{2,10},{10... | collective-permute-start | bytes 1966088 | tf_op jit(solution)/shard_map/ppermute | solution.py:28
  118.6 35.0 %collective-permute-start.11 = (bf16[1280,256]{1,0:T(8,128)(2,1)}, bf16[1280,256]{1,0:T(8,128)(2,1)S(1)}, u32[]{:S(2)}, u32[]{:S(2)}) collective-permute-start(bf16[1280,256]{1,0:T(8,128)(2,1)} %project.2.refs_5_), channel_id=1, source_target_pairs={{0,16},{8,24},{16,0},{24,8},{1,17},{9,25},{17,1},{25,9},{2,18},{10... | collective-permute-start | bytes 1966088 | tf_op jit(solution)/shard_map/ppermute | solution.py:28
  120.7 32.8 %collective-permute-start.10 = (bf16[1280,256]{1,0:T(8,128)(2,1)}, bf16[1280,256]{1,0:T(8,128)(2,1)}, u32[]{:S(2)}, u32[]{:S(2)}) collective-permute-start(bf16[1280,256]{1,0:T(8,128)(2,1)} %project.2.refs_5_), channel_id=1, source_target_pairs={{0,24},{8,0},{16,8},{24,16},{1,25},{9,1},{17,9},{25,17},{2,26},{10... | collective-permute-start | bytes 1966088 | tf_op jit(solution)/shard_map/ppermute | solution.py:28
  133.9 29.3 %collective-permute-start.15 = (bf16[1280,256]{1,0:T(8,128)(2,1)}, bf16[1280,256]{1,0:T(8,128)(2,1)S(1)}, u32[]{:S(2)}, u32[]{:S(2)}) collective-permute-start(bf16[1280,256]{1,0:T(8,128)(2,1)} %project.3.refs_5_), channel_id=1, source_target_pairs={{0,2},{2,4},{4,6},{6,0},{1,3},{3,5},{5,7},{7,1},{8,10},{10,12},{12... | collective-permute-start | bytes 1966088 | tf_op jit(solution)/shard_map/ppermute | solution.py:28
  135.2 31.5 %collective-permute-start.14 = (bf16[1280,256]{1,0:T(8,128)(2,1)}, bf16[1280,256]{1,0:T(8,128)(2,1)S(1)}, u32[]{:S(2)}, u32[]{:S(2)}) collective-permute-start(bf16[1280,256]{1,0:T(8,128)(2,1)} %project.3.refs_5_), channel_id=1, source_target_pairs={{0,4},{2,6},{4,0},{6,2},{1,5},{3,7},{5,1},{7,3},{8,12},{10,14},{12... | collective-permute-start | bytes 1966088 | tf_op jit(solution)/shard_map/ppermute | solution.py:28
  148.8 19.0 %collective-permute-start.13 = (bf16[1280,256]{1,0:T(8,128)(2,1)}, bf16[1280,256]{1,0:T(8,128)(2,1)S(1)}, u32[]{:S(2)}, u32[]{:S(2)}) collective-permute-start(bf16[1280,256]{1,0:T(8,128)(2,1)} %project.3.refs_5_), channel_id=1, source_target_pairs={{0,6},{2,0},{4,2},{6,4},{1,7},{3,1},{5,3},{7,5},{8,14},{10,8},{12,... | collective-permute-start | bytes 1966088 | tf_op jit(solution)/shard_map/ppermute | solution.py:28
  189.6 80.6 %reduce-scatter.5.cloned.1.call-start = ((), (), s32[]{:S(2)}) async-start(), calls=%async_computation.5 | async-start | bytes 2621440 | tf_op jit(solution)/shard_map/reduce_scatter | solution.py:397
  214.2 29.3 %collective-permute-start.22 = (bf16[1280,256]{1,0:T(8,128)(2,1)}, bf16[1280,256]{1,0:T(8,128)(2,1)S(1)}, u32[]{:S(2)}, u32[]{:S(2)}) collective-permute-start(bf16[1280,256]{1,0:T(8,128)(2,1)} %get-tuple-element.38), channel_id=1, source_target_pairs={{0,2},{2,4},{4,6},{6,0},{1,3},{3,5},{5,7},{7,1},{8,10},{10,12},{12... | collective-permute-start | bytes 1966088 | tf_op jit(solution)/shard_map/ppermute | solution.py:28
  217.2 26.2 %collective-permute-start.23 = (bf16[1280,256]{1,0:T(8,128)(2,1)}, bf16[1280,256]{1,0:T(8,128)(2,1)S(1)}, u32[]{:S(2)}, u32[]{:S(2)}) collective-permute-start(bf16[1280,256]{1,0:T(8,128)(2,1)} %get-tuple-element.39), channel_id=1, source_target_pairs={{0,6},{2,0},{4,2},{6,4},{1,7},{3,1},{5,3},{7,5},{8,14},{10,8},{12,... | collective-permute-start | bytes 1966088 | tf_op jit(solution)/shard_map/ppermute | solution.py:28
  217.5 26.0 %collective-permute-start.24 = (bf16[1280,256]{1,0:T(8,128)(2,1)S(1)}, bf16[1280,256]{1,0:T(8,128)(2,1)S(1)}, u32[]{:S(2)}, u32[]{:S(2)}) collective-permute-start(bf16[1280,256]{1,0:T(8,128)(2,1)S(1)} %copy-done.23), channel_id=1, source_target_pairs={{0,4},{2,6},{4,0},{6,2},{1,5},{3,7},{5,1},{7,3},{8,12},{10,14},{12... | collective-permute-start | bytes 1966088 | tf_op jit(solution)/shard_map/ppermute | solution.py:28
  243.8 26.1 %collective-permute-start.25 = (bf16[2048,128]{1,0:T(8,128)(2,1)}, bf16[2048,128]{1,0:T(8,128)(2,1)S(1)}, u32[]{:S(2)}, u32[]{:S(2)}) collective-permute-start(bf16[2048,128]{1,0:T(8,128)(2,1)} %get-tuple-element.42), channel_id=1, source_target_pairs={{0,2},{2,4},{4,6},{6,0},{1,3},{3,5},{5,7},{7,1},{8,10},{10,12},{12... | collective-permute-start | bytes 1572872 | tf_op jit(solution)/shard_map/ppermute | solution.py:28
  244.7 25.2 %collective-permute-start.26 = (bf16[2048,128]{1,0:T(8,128)(2,1)}, bf16[2048,128]{1,0:T(8,128)(2,1)S(1)}, u32[]{:S(2)}, u32[]{:S(2)}) collective-permute-start(bf16[2048,128]{1,0:T(8,128)(2,1)} %get-tuple-element.43), channel_id=1, source_target_pairs={{0,6},{2,0},{4,2},{6,4},{1,7},{3,1},{5,3},{7,5},{8,14},{10,8},{12,... | collective-permute-start | bytes 1572872 | tf_op jit(solution)/shard_map/ppermute | solution.py:28
  247.1 22.8 %collective-permute-start.27 = (bf16[2048,128]{1,0:T(8,128)(2,1)}, bf16[2048,128]{1,0:T(8,128)(2,1)S(1)}, u32[]{:S(2)}, u32[]{:S(2)}) collective-permute-start(bf16[2048,128]{1,0:T(8,128)(2,1)} %get-tuple-element.44), channel_id=1, source_target_pairs={{0,4},{2,6},{4,0},{6,2},{1,5},{3,7},{5,1},{7,3},{8,12},{10,14},{12... | collective-permute-start | bytes 1572872 | tf_op jit(solution)/shard_map/ppermute | solution.py:28
  (35 other events, 316.9 us)
Sparse Core Ops, SparseCore 0:
  10.9 92.7 all-gather.1
  189.8 34.3 reduce-scatter.2
  226.6 29.4 reduce-scatter.4

commit v3 on v2

--- a/solution.py
+++ b/solution.py
@@ -375,15 +375,14 @@
 
     q_a = ring_gather(qg[0], "y")
     q_b = ring_gather(qg[1], "z")
-    rings = (q_a[2], q_a[3], q_b[2], q_b[3])
-    names = gather_small(tie(neighbours.reshape(-1), rings), ("z", "y", "c")).reshape(RING, RING, 2, -1)
-    ready = tie(weight, names)
+    names = gather_small(tie(neighbours.reshape(-1), (q_a[1], q_a[4], q_b[1], q_b[4])), ("z", "y", "c")).reshape(RING, RING, 2, -1)
     names = jnp.where(c == 0, names, names[:, :, ::-1])
     names_a = relative(lax.dynamic_index_in_dim(names, z, 0, False), y).reshape(2 * RING, -1)
     names_b = relative(lax.dynamic_index_in_dim(names, y, 1, False), z).reshape(2 * RING, -1)
     table_a = unit_table(names_a, y, z, c, block_count, False)
     table_b = unit_table(names_b, z, y, c, block_count, True)
 
+    ready = tie(weight, (table_a, table_b, q_a, q_b))
     kv_a = line_gather(project(ready, 2 * c, states, states_mate), "z")
     kv_b = line_gather(project(ready, 2 * c + 1, states, states_mate), "y")
 

time: 284 us -> 283 us (level)
  waiting for transfers between devices: 102 us -> 86.4 us
  starting transfers between devices: 50.9 us -> 62.3 us
  local copies, waits for them, and re-layouts: 16.3 us -> 19.8 us
    ppermute x26, waiting for transfers between devices: 89.6 us -> 74.5 us  [shift(): return lax.ppermute(x, axis, [(i, (i + by) % RING) for i in range(RING)])]
    ppermute x26, starting transfers between devices: 44.1 us -> 54.9 us  [shift(): return lax.ppermute(x, axis, [(i, (i + by) % RING) for i in range(RING)])]
    all_to_all x1, waiting for transfers between devices: 6.93 us -> 0.01 us  [gather_small(): lax.all_to_all(jnp.broadcast_to(x[None], (count, *x.shape)), axes, 0, 0,...]
    all_gather x1, waiting for transfers between devices: 0.02 us -> 6.43 us  [on_device(): lax.all_gather(jnp.concatenate([key_weight, value_weight], axis=1), ('z',...]
  transfers between devices with their start and end apart: 35 -> 35, of which waited for: 15 -> 19; matrix products, arithmetic and copies ran while one was open for 8% -> 10% of each run, Pallas kernels for 20% -> 19%
where the time goes in v3:
time: 283 us; the launch traced here: 279 us
  waiting for transfers between devices  86.4 us (31%)
  Pallas kernels  78.7 us (28%)
  starting transfers between devices  62.3 us (22%)
  local copies, waits for them, and re-layouts  19.8 us (7%)
  other arithmetic  17.8 us (6%)
  between operations  14.4 us (5%)
    ppermute x26, waiting for transfers between devices, shift(): return lax.ppermute(x, axis, [(i, (i + by) % RING) for i in range(RING)])  74.5 us
    ppermute x26, starting transfers between devices, shift(): return lax.ppermute(x, axis, [(i, (i + by) % RING) for i in range(RING)])  54.9 us
    pallas_call x2, Pallas kernels, call_grads(): pl.pallas_call(functools.partial(grads_kernel, ctx_ring, kvg_ring), out_s...  25.4 us
    pallas_call x2, Pallas kernels, project(): pl.pallas_call(project_kernel, grid_spec=pltpu.PrefetchScalarGridSpec(num...  23.8 us
    pallas_call x1, Pallas kernels, expand(): pl.pallas_call(expand_kernel, grid=(4,), out_shape=jax.ShapeDtypeStruct((...  16.3 us
    pallas_call x2, Pallas kernels, call_stats(): pl.pallas_call(stats_kernel, out_shape=jax.ShapeDtypeStruct((UNITS + 1, 2...  13.1 us
    all_gather x1, waiting for transfers between devices, on_device(): lax.all_gather(jnp.concatenate([key_weight, value_weight], axis=1), ('z',...  6.43 us
    all_to_all x1, starting transfers between devices, gather_small(): lax.all_to_all(jnp.broadcast_to(x[None], (count, *x.shape)), axes, 0, 0,...  6.03 us
  transfers between devices with their start and end apart: 35, of which 19 were waited for; matrix products, arithmetic and copies ran while one was open for 10% of the time, Pallas kernels for 19%

profile of v3, /device:TPU:0, one launch (start us, length us, event | category | flops | bytes accessed | tf_op | source)
XLA Modules:
  0.0 279.4 jit_solution(9278301707908343726)
XLA Ops:
  9.9 2.6 collective-permute-done
  20.9 27.4 %collective-permute-done.2.refs_4_ = bf16[2048,256]{1,0:T(8,128)(2,1)} collective-permute-done((bf16[2048,256]{1,0:T(8,128)(2,1)S(1)}, bf16[2048,256]{1,0:T(8,128)(2,1)}, u32[]{:S(2)}, u32[]{:S(2)}) %collective-permute-start.2) | collective-permute-done | bytes 1048608 | tf_op jit(solution)/shard_map/ppermute | solution.py:28
  48.3 3.9 %collective-permute-done.4.refs_4_ = bf16[2048,256]{1,0:T(8,128)(2,1)S(1)} collective-permute-done((bf16[2048,256]{1,0:T(8,128)(2,1)S(1)}, bf16[2048,256]{1,0:T(8,128)(2,1)S(1)}, u32[]{:S(2)}, u32[]{:S(2)}) %collective-permute-start.4) | collective-permute-done | bytes 1048608 | tf_op jit(solution)/shard_map/ppermute | solution.py:28
  52.9 6.0 %all-to-all-start = ((s32[32,1,32]{2,1,0:T(1,128)}), s32[32,1,32]{2,1,0:T(1,128)S(1)}, u32[]{:S(2)}, u32[]{:S(2)}) async-start(s32[32,1,32]{2,1,0:T(1,128)} %broadcast_in_dim.207), calls=%async_computation | async-start | bytes 32768 | tf_op jit(solution)/shard_map/all_to_all | solution.py:41
  88.6 2.3 collective-permute-done.5.refs_2_
  90.9 3.4 %collective-permute-done.8.refs_3_ = bf16[1024,256]{1,0:T(8,128)(2,1)S(1)} collective-permute-done((bf16[1024,256]{1,0:T(8,128)(2,1)}, bf16[1024,256]{1,0:T(8,128)(2,1)S(1)}, u32[]{:S(2)}, u32[]{:S(2)}) %collective-permute-start.8) | collective-permute-done | bytes 524320 | tf_op jit(solution)/shard_map/ppermute | solution.py:28
  96.7 6.4 %all-gather.2.cloned.1.call-done.w_key.w_value.refs_4_ = bf16[8192,1024]{1,0:T(8,128)(2,1)} async-done(((bf16[256,1024]{1,0:T(8,128)(2,1)}), bf16[8192,1024]{1,0:T(8,128)(2,1)}) %all-gather.2.cloned.1.call-update) | async-done | bytes 16777232 | tf_op jit(solution)/shard_map/all_gather | solution.py:366
  103.1 11.9 %project.2.refs_5_ = bf16[1280,256]{1,0:T(8,128)(2,1)} custom-call(s32[1]{0:T(128)} %bitcast.19.head, bf16[8192,1024]{1,0:T(8,128)(2,1)} %all-gather.2.cloned.1.call-done.w_key.w_value.refs_4_, bf16[8192,1024]{1,0:T(8,128)(2,1)} %all-gather.2.cloned.1.call-done.w_key.w_value.refs_4_, bf16[640,8192]{1,0:T(8,128)(2,1)} %bitcast.36, ...), custom_call_target="tpu_custom_call" | custom-call | tf_op jit(solution)/shard_map/project/pallas_call | solution.py:154
  116.0 2.9 %collective-permute-start.11 = (bf16[1280,256]{1,0:T(8,128)(2,1)}, bf16[1280,256]{1,0:T(8,128)(2,1)S(1)}, u32[]{:S(2)}, u32[]{:S(2)}) collective-permute-start(bf16[1280,256]{1,0:T(8,128)(2,1)} %project.2.refs_5_), channel_id=1, source_target_pairs={{0,16},{8,24},{16,0},{24,8},{1,17},{9,25},{17,1},{25,9},{2,18},{10... | collective-permute-start | bytes 1966088 | tf_op jit(solution)/shard_map/ppermute | solution.py:28
  120.2 11.9 %project.3.refs_5_ = bf16[1280,256]{1,0:T(8,128)(2,1)} custom-call(s32[1]{0:T(128)} %bitcast.21.head, bf16[8192,1024]{1,0:T(8,128)(2,1)} %all-gather.2.cloned.1.call-done.w_key.w_value.refs_4_, bf16[8192,1024]{1,0:T(8,128)(2,1)} %all-gather.2.cloned.1.call-done.w_key.w_value.refs_4_, bf16[640,8192]{1,0:T(8,128)(2,1)} %bitcast.37, ...), custom_call_target="tpu_custom_call" | custom-call | tf_op jit(solution)/shard_map/project/pallas_call | solution.py:154
  132.4 2.7 collective-permute-start.14
  135.1 15.1 %collective-permute-start.13 = (bf16[1280,256]{1,0:T(8,128)(2,1)}, bf16[1280,256]{1,0:T(8,128)(2,1)S(1)}, u32[]{:S(2)}, u32[]{:S(2)}) collective-permute-start(bf16[1280,256]{1,0:T(8,128)(2,1)} %project.3.refs_5_), channel_id=1, source_target_pairs={{0,6},{2,0},{4,2},{6,4},{1,7},{3,1},{5,3},{7,5},{8,14},{10,8},{12,... | collective-permute-start | bytes 1966088 | tf_op jit(solution)/shard_map/ppermute | solution.py:28
  151.0 6.5 %pair_stats.2.refs_9_ = f32[65,2,128]{2,1,0:T(2,128)} custom-call(s32[515]{0:T(1024)} %pad_add_fusion.table, bf16[2048,256]{1,0:T(8,128)(2,1)} %copy-done.1, bf16[2048,256]{1,0:T(8,128)(2,1)} %collective-permute-done.1.refs_1_, bf16[1024,256]{1,0:T(8,128)(2,1)} %collective-permute-done.5.refs_2_, bf16[1024,256]{1,0:T(8,128)(2,1)} %collective-permute-done.6.refs_3_, ...), custom_call_target="tpu_custom_call" | custom-call | tf_op jit(solution)/shard_map/pair_stats/pallas_call | solution.py:312
  157.9 2.8 %collective-permute-start.17 = (f32[65,2,128]{2,1,0:T(2,128)}, f32[65,2,128]{2,1,0:T(2,128)S(1)}, u32[]{:S(2)}, u32[]{:S(2)}) collective-permute-start(f32[65,2,128]{2,1,0:T(2,128)} %pair_stats.2.refs_9_), channel_id=1, source_target_pairs={{0,4},{2,6},{4,0},{6,2},{1,5},{3,7},{5,1},{7,3},{8,12},{10,14},{12... | collective-permute-start | bytes 199688 | tf_op jit(solution)/shard_map/ppermute | solution.py:28
  162.5 2.3 collective-permute-done.14.refs_7_
  167.1 6.5 %pair_stats.3.refs_9_ = f32[65,2,128]{2,1,0:T(2,128)} custom-call(s32[515]{0:T(1024)} %pad_add_fusion.1.table, bf16[2048,256]{1,0:T(8,128)(2,1)} %copy-done, bf16[2048,256]{1,0:T(8,128)(2,1)} %collective-permute-done.3.refs_1_, bf16[1024,256]{1,0:T(8,128)(2,1)} %copy-done.9, bf16[1024,256]{1,0:T(8,128)(2,1)} %copy-done.8, bf16[2048,256]{1,0:T(8,128)(2,1)} %copy-done.2, ...), custom_call_target="tpu_custom_call" | custom-call | tf_op jit(solution)/shard_map/pair_stats/pallas_call | solution.py:312
  174.9 12.5 %pair_grads.2 = (f32[2048,128]{1,0:T(8,128)}, bf16[2048,128]{1,0:T(8,128)(2,1)}, bf16[2048,128]{1,0:T(8,128)(2,1)}, bf16[2048,128]{1,0:T(8,128)(2,1)}, bf16[5120,256]{1,0:T(8,128)(2,1)}) custom-call(s32[515]{0:T(1024)} %pad_add_fusion.table, bf16[2048,256]{1,0:T(8,128)(2,1)} %copy-done.1, bf16[2048,256]{1,0:T(8,128)(2,1)} %collective-permute-done.1.refs_1_, ...), custom_call_target="tpu_custom_call" | custom-call | tf_op jit(solution)/shard_map/pair_grads/pallas_call | solution.py:337
  190.6 2.6 collective-permute-start.19
  196.1 12.9 %pair_grads.3 = (bf16[8192,128]{1,0:T(8,128)(2,1)}, f32[1280,256]{1,0:T(8,128)}, bf16[1280,256]{1,0:T(8,128)(2,1)}, bf16[1280,256]{1,0:T(8,128)(2,1)}, bf16[1280,256]{1,0:T(8,128)(2,1)}) custom-call(s32[515]{0:T(1024)} %pad_add_fusion.1.table, bf16[2048,256]{1,0:T(8,128)(2,1)} %copy-done, bf16[2048,256]{1,0:T(8,128)(2,1)} %collective-permute-done.3.refs_1_, ...), custom_call_target="tpu_custom_call" | custom-call | tf_op jit(solution)/shard_map/pair_grads/pallas_call | solution.py:337
  209.0 3.3 %collective-permute-start.22 = (bf16[1280,256]{1,0:T(8,128)(2,1)}, bf16[1280,256]{1,0:T(8,128)(2,1)S(1)}, u32[]{:S(2)}, u32[]{:S(2)}) collective-permute-start(bf16[1280,256]{1,0:T(8,128)(2,1)} %get-tuple-element.38), channel_id=1, source_target_pairs={{0,2},{2,4},{4,6},{6,0},{1,3},{3,5},{5,7},{7,1},{8,10},{10,12},{12... | collective-permute-start | bytes 1966088 | tf_op jit(solution)/shard_map/ppermute | solution.py:28
  215.4 13.5 %collective-permute-done.22 = bf16[1280,256]{1,0:T(8,128)(2,1)S(1)} collective-permute-done((bf16[1280,256]{1,0:T(8,128)(2,1)}, bf16[1280,256]{1,0:T(8,128)(2,1)S(1)}, u32[]{:S(2)}, u32[]{:S(2)}) %collective-permute-start.22) | collective-permute-done | bytes 655392 | tf_op jit(solution)/shard_map/ppermute | solution.py:28
  228.9 10.9 %collective-permute-done.23 = bf16[1280,256]{1,0:T(8,128)(2,1)S(1)} collective-permute-done((bf16[1280,256]{1,0:T(8,128)(2,1)}, bf16[1280,256]{1,0:T(8,128)(2,1)S(1)}, u32[]{:S(2)}, u32[]{:S(2)}) %collective-permute-start.23) | collective-permute-done | bytes 655392 | tf_op jit(solution)/shard_map/ppermute | solution.py:28
  243.1 2.6 collective-permute-start.26
  250.9 16.3 %expand.1 = bf16[640,8192]{1,0:T(8,128)(2,1)} custom-call(s32[1]{0:T(128)} %bitcast.22.core, bf16[640,256]{1,0:T(8,128)(2,1)} %get-tuple-element.97.refs_0_, bf16[640,256]{1,0:T(8,128)(2,1)} %get-tuple-element.95.refs_1_, bf16[640,256]{1,0:T(8,128)(2,1)} %copy-done.15, bf16[640,256]{1,0:T(8,128)(2,1)} %copy-done.14, ...), custom_call_target="tpu_custom_call" | custom-call | tf_op jit(solution)/shard_map/expand/pallas_call | solution.py:193
  (220 shorter events, 75.5 us)
Async XLA Ops:
  7.2 95.9 %all-gather.2.cloned.1.call-start = ((), (), s32[]{:S(2)}) async-start(), calls=%async_computation.3 | async-start | bytes 17301504 | tf_op jit(solution)/shard_map/all_gather | solution.py:366
  12.6 90.5 %collective-permute-start.9 = (bf16[640,8192]{1,0:T(8,128)(2,1)}, bf16[640,8192]{1,0:T(8,128)(2,1)}, u32[]{:S(2)}, u32[]{:S(2)}) collective-permute-start(bf16[640,8192]{1,0:T(8,128)(2,1)} %bitcast.35), channel_id=1, source_target_pairs={{0,1},{1,0},{2,3},{3,2},{4,5},{5,4},{6,7},{7,6},{8,9},{9,8},{10,11... | collective-permute-start | bytes 31457288 | tf_op jit(solution)/shard_map/ppermute | solution.py:32
  12.9 35.4 %collective-permute-start.2 = (bf16[2048,256]{1,0:T(8,128)(2,1)S(1)}, bf16[2048,256]{1,0:T(8,128)(2,1)}, u32[]{:S(2)}, u32[]{:S(2)}) collective-permute-start(bf16[2048,256]{1,0:T(8,128)(2,1)S(1)} %pad_maximum_fusion.1.refs_0_), channel_id=1, source_target_pairs={{0,2},{2,4},{4,6},{6,0},{1,3},{3,5},{5,7},{7,1},{8,10},{10,12},{12... | collective-permute-start | bytes 3145736 | tf_op jit(solution)/shard_map/ppermute | solution.py:28
  14.7 33.7 %collective-permute-start.1 = (bf16[2048,256]{1,0:T(8,128)(2,1)S(1)}, bf16[2048,256]{1,0:T(8,128)(2,1)}, u32[]{:S(2)}, u32[]{:S(2)}) collective-permute-start(bf16[2048,256]{1,0:T(8,128)(2,1)S(1)} %pad_maximum_fusion.1.refs_0_), channel_id=1, source_target_pairs={{0,6},{2,0},{4,2},{6,4},{1,7},{3,1},{5,3},{7,5},{8,14},{10,8},{12,... | collective-permute-start | bytes 3145736 | tf_op jit(solution)/shard_map/ppermute | solution.py:28
  16.4 35.9 %collective-permute-start.4 = (bf16[2048,256]{1,0:T(8,128)(2,1)S(1)}, bf16[2048,256]{1,0:T(8,128)(2,1)S(1)}, u32[]{:S(2)}, u32[]{:S(2)}) collective-permute-start(bf16[2048,256]{1,0:T(8,128)(2,1)S(1)} %pad_maximum_fusion.2.refs_0_), channel_id=1, source_target_pairs={{0,8},{8,16},{16,24},{24,0},{1,9},{9,17},{17,25},{25,1},{2,10},{10... | collective-permute-start | bytes 3145736 | tf_op jit(solution)/shard_map/ppermute | solution.py:28
  18.4 33.8 %collective-permute-start.3 = (bf16[2048,256]{1,0:T(8,128)(2,1)S(1)}, bf16[2048,256]{1,0:T(8,128)(2,1)}, u32[]{:S(2)}, u32[]{:S(2)}) collective-permute-start(bf16[2048,256]{1,0:T(8,128)(2,1)S(1)} %pad_maximum_fusion.2.refs_0_), channel_id=1, source_target_pairs={{0,24},{8,0},{16,8},{24,16},{1,25},{9,1},{17,9},{25,17},{2,26},{10... | collective-permute-start | bytes 3145736 | tf_op jit(solution)/shard_map/ppermute | solution.py:28
  58.9 187.6 %reduce-scatter.3.cloned.1.call-start = ((), (), s32[]{:S(2)}) async-start(), calls=%async_computation.4 | async-start | bytes 3276800 | tf_op jit(solution)/shard_map/reduce_scatter | solution.py:394
  61.3 27.3 %collective-permute-start.6 = (bf16[1024,256]{1,0:T(8,128)(2,1)}, bf16[1024,256]{1,0:T(8,128)(2,1)}, u32[]{:S(2)}, u32[]{:S(2)}) collective-permute-start(bf16[1024,256]{1,0:T(8,128)(2,1)} %slice.51), channel_id=1, source_target_pairs={{0,2},{2,4},{4,6},{6,0},{1,3},{3,5},{5,7},{7,1},{8,10},{10,12},{12... | collective-permute-start | bytes 1572872 | tf_op jit(solution)/shard_map/ppermute | solution.py:28
  65.0 25.9 %collective-permute-start.5 = (bf16[1024,256]{1,0:T(8,128)(2,1)}, bf16[1024,256]{1,0:T(8,128)(2,1)}, u32[]{:S(2)}, u32[]{:S(2)}) collective-permute-start(bf16[1024,256]{1,0:T(8,128)(2,1)} %slice.50), channel_id=1, source_target_pairs={{0,6},{2,0},{4,2},{6,4},{1,7},{3,1},{5,3},{7,5},{8,14},{10,8},{12,... | collective-permute-start | bytes 1572872 | tf_op jit(solution)/shard_map/ppermute | solution.py:28
  67.3 27.0 %collective-permute-start.8 = (bf16[1024,256]{1,0:T(8,128)(2,1)}, bf16[1024,256]{1,0:T(8,128)(2,1)S(1)}, u32[]{:S(2)}, u32[]{:S(2)}) collective-permute-start(bf16[1024,256]{1,0:T(8,128)(2,1)} %slice.53), channel_id=1, source_target_pairs={{0,8},{8,16},{16,24},{24,0},{1,9},{9,17},{17,25},{25,1},{2,10},{10... | collective-permute-start | bytes 1572872 | tf_op jit(solution)/shard_map/ppermute | solution.py:28
  71.0 25.6 %collective-permute-start.7 = (bf16[1024,256]{1,0:T(8,128)(2,1)}, bf16[1024,256]{1,0:T(8,128)(2,1)S(1)}, u32[]{:S(2)}, u32[]{:S(2)}) collective-permute-start(bf16[1024,256]{1,0:T(8,128)(2,1)} %slice.52), channel_id=1, source_target_pairs={{0,24},{8,0},{16,8},{24,16},{1,25},{9,1},{17,9},{25,17},{2,26},{10... | collective-permute-start | bytes 1572872 | tf_op jit(solution)/shard_map/ppermute | solution.py:28
  115.0 20.0 %collective-permute-start.12 = (bf16[1280,256]{1,0:T(8,128)(2,1)}, bf16[1280,256]{1,0:T(8,128)(2,1)S(1)}, u32[]{:S(2)}, u32[]{:S(2)}) collective-permute-start(bf16[1280,256]{1,0:T(8,128)(2,1)} %project.2.refs_5_), channel_id=1, source_target_pairs={{0,8},{8,16},{16,24},{24,0},{1,9},{9,17},{17,25},{25,1},{2,10},{10... | collective-permute-start | bytes 1966088 | tf_op jit(solution)/shard_map/ppermute | solution.py:28
  116.0 34.2 %collective-permute-start.11 = (bf16[1280,256]{1,0:T(8,128)(2,1)}, bf16[1280,256]{1,0:T(8,128)(2,1)S(1)}, u32[]{:S(2)}, u32[]{:S(2)}) collective-permute-start(bf16[1280,256]{1,0:T(8,128)(2,1)} %project.2.refs_5_), channel_id=1, source_target_pairs={{0,16},{8,24},{16,0},{24,8},{1,17},{9,25},{17,1},{25,9},{2,18},{10... | collective-permute-start | bytes 1966088 | tf_op jit(solution)/shard_map/ppermute | solution.py:28
  118.9 31.3 %collective-permute-start.10 = (bf16[1280,256]{1,0:T(8,128)(2,1)}, bf16[1280,256]{1,0:T(8,128)(2,1)}, u32[]{:S(2)}, u32[]{:S(2)}) collective-permute-start(bf16[1280,256]{1,0:T(8,128)(2,1)} %project.2.refs_5_), channel_id=1, source_target_pairs={{0,24},{8,0},{16,8},{24,16},{1,25},{9,1},{17,9},{25,17},{2,26},{10... | collective-permute-start | bytes 1966088 | tf_op jit(solution)/shard_map/ppermute | solution.py:28
  132.1 30.4 %collective-permute-start.15 = (bf16[1280,256]{1,0:T(8,128)(2,1)}, bf16[1280,256]{1,0:T(8,128)(2,1)S(1)}, u32[]{:S(2)}, u32[]{:S(2)}) collective-permute-start(bf16[1280,256]{1,0:T(8,128)(2,1)} %project.3.refs_5_), channel_id=1, source_target_pairs={{0,2},{2,4},{4,6},{6,0},{1,3},{3,5},{5,7},{7,1},{8,10},{10,12},{12... | collective-permute-start | bytes 1966088 | tf_op jit(solution)/shard_map/ppermute | solution.py:28
  132.4 32.5 %collective-permute-start.14 = (bf16[1280,256]{1,0:T(8,128)(2,1)}, bf16[1280,256]{1,0:T(8,128)(2,1)S(1)}, u32[]{:S(2)}, u32[]{:S(2)}) collective-permute-start(bf16[1280,256]{1,0:T(8,128)(2,1)} %project.3.refs_5_), channel_id=1, source_target_pairs={{0,4},{2,6},{4,0},{6,2},{1,5},{3,7},{5,1},{7,3},{8,12},{10,14},{12... | collective-permute-start | bytes 1966088 | tf_op jit(solution)/shard_map/ppermute | solution.py:28
  135.1 31.2 %collective-permute-start.13 = (bf16[1280,256]{1,0:T(8,128)(2,1)}, bf16[1280,256]{1,0:T(8,128)(2,1)S(1)}, u32[]{:S(2)}, u32[]{:S(2)}) collective-permute-start(bf16[1280,256]{1,0:T(8,128)(2,1)} %project.3.refs_5_), channel_id=1, source_target_pairs={{0,6},{2,0},{4,2},{6,4},{1,7},{3,1},{5,3},{7,5},{8,14},{10,8},{12,... | collective-permute-start | bytes 1966088 | tf_op jit(solution)/shard_map/ppermute | solution.py:28
  187.5 80.1 %reduce-scatter.5.cloned.1.call-start = ((), (), s32[]{:S(2)}) async-start(), calls=%async_computation.5 | async-start | bytes 2621440 | tf_op jit(solution)/shard_map/reduce_scatter | solution.py:396
  209.0 19.9 %collective-permute-start.22 = (bf16[1280,256]{1,0:T(8,128)(2,1)}, bf16[1280,256]{1,0:T(8,128)(2,1)S(1)}, u32[]{:S(2)}, u32[]{:S(2)}) collective-permute-start(bf16[1280,256]{1,0:T(8,128)(2,1)} %get-tuple-element.38), channel_id=1, source_target_pairs={{0,2},{2,4},{4,6},{6,0},{1,3},{3,5},{5,7},{7,1},{8,10},{10,12},{12... | collective-permute-start | bytes 1966088 | tf_op jit(solution)/shard_map/ppermute | solution.py:28
  212.3 27.5 %collective-permute-start.23 = (bf16[1280,256]{1,0:T(8,128)(2,1)}, bf16[1280,256]{1,0:T(8,128)(2,1)S(1)}, u32[]{:S(2)}, u32[]{:S(2)}) collective-permute-start(bf16[1280,256]{1,0:T(8,128)(2,1)} %get-tuple-element.39), channel_id=1, source_target_pairs={{0,6},{2,0},{4,2},{6,4},{1,7},{3,1},{5,3},{7,5},{8,14},{10,8},{12,... | collective-permute-start | bytes 1966088 | tf_op jit(solution)/shard_map/ppermute | solution.py:28
  214.0 28.1 %collective-permute-start.24 = (bf16[1280,256]{1,0:T(8,128)(2,1)S(1)}, bf16[1280,256]{1,0:T(8,128)(2,1)S(1)}, u32[]{:S(2)}, u32[]{:S(2)}) collective-permute-start(bf16[1280,256]{1,0:T(8,128)(2,1)S(1)} %copy-done.25), channel_id=1, source_target_pairs={{0,4},{2,6},{4,0},{6,2},{1,5},{3,7},{5,1},{7,3},{8,12},{10,14},{12... | collective-permute-start | bytes 1966088 | tf_op jit(solution)/shard_map/ppermute | solution.py:28
  242.4 24.8 %collective-permute-start.25 = (bf16[2048,128]{1,0:T(8,128)(2,1)}, bf16[2048,128]{1,0:T(8,128)(2,1)S(1)}, u32[]{:S(2)}, u32[]{:S(2)}) collective-permute-start(bf16[2048,128]{1,0:T(8,128)(2,1)} %get-tuple-element.42), channel_id=1, source_target_pairs={{0,2},{2,4},{4,6},{6,0},{1,3},{3,5},{5,7},{7,1},{8,10},{10,12},{12... | collective-permute-start | bytes 1572872 | tf_op jit(solution)/shard_map/ppermute | solution.py:28
  243.1 24.1 %collective-permute-start.26 = (bf16[2048,128]{1,0:T(8,128)(2,1)}, bf16[2048,128]{1,0:T(8,128)(2,1)S(1)}, u32[]{:S(2)}, u32[]{:S(2)}) collective-permute-start(bf16[2048,128]{1,0:T(8,128)(2,1)} %get-tuple-element.43), channel_id=1, source_target_pairs={{0,6},{2,0},{4,2},{6,4},{1,7},{3,1},{5,3},{7,5},{8,14},{10,8},{12,... | collective-permute-start | bytes 1572872 | tf_op jit(solution)/shard_map/ppermute | solution.py:28
  245.7 21.5 %collective-permute-start.27 = (bf16[2048,128]{1,0:T(8,128)(2,1)}, bf16[2048,128]{1,0:T(8,128)(2,1)S(1)}, u32[]{:S(2)}, u32[]{:S(2)}) collective-permute-start(bf16[2048,128]{1,0:T(8,128)(2,1)} %get-tuple-element.44), channel_id=1, source_target_pairs={{0,4},{2,6},{4,0},{6,2},{1,5},{3,7},{5,1},{7,3},{8,12},{10,14},{12... | collective-permute-start | bytes 1572872 | tf_op jit(solution)/shard_map/ppermute | solution.py:28
  (37 other events, 356.5 us)
Sparse Core Ops, SparseCore 0:
  10.3 92.7 all-gather.1
  187.6 35.1 reduce-scatter.2
  225.2 29.4 reduce-scatter.4
